TPU v7x, 128 devices: a whole 4x4x4 slice. The times are simulated.
128 devices in a mesh: var: 8 (over z, x_hi), patch: 8 (over y, core), win: 2 (over x_lo).
Axes of the slice: x: 4 (x_hi: 2, x_lo: 2; x = x_hi * 2 + x_lo), y: 4, z: 4, core: 2. Of those that a mesh axis runs over, the one named last changes fastest.
Arguments:
- fields: bfloat16 [480, 16, 1024], P(('win', 'var'), 'patch'), parts along dimension 0, may hold values from -6 to 6
- var_ids: int32 [240], replicated, may hold values from 0 to 239, each once
- level_of: int32 [240], replicated, may hold values from 0 to 37
- window_offset: int32 [2], P('win'), parts along dimension 0, may hold values from 0 to 164
- w_embed: bfloat16 [240, 16, 512], replicated, may hold values from -1.5 to 1.5
- var_emb: bfloat16 [240, 512], replicated, may hold values from -6 to 6
- w_key: bfloat16 [512, 512], replicated, may hold values from -0.25 to 0.25
- w_value: bfloat16 [512, 512], replicated, may hold values from -0.25 to 0.25
- w_out: bfloat16 [512, 512], replicated, may hold values from -0.25 to 0.25
- latent_query: float32 [8, 64], replicated, may hold values from -9 to 9
- bias_table: float32 [38, 8], replicated, may hold values from -4 to 300
- lat_emb: bfloat16 [180, 512], replicated, may hold values from -3 to 3
- d_aggregated: bfloat16 [32, 64, 512], P('win', ('var', 'patch')), parts along dimension 0, may hold values from -6 to 6
Outputs:
- aggregated: bfloat16 [32, 64, 512], P('win', ('var', 'patch')), parts along dimension 0
- embed_grad_rows: float32 [480, 16, 512], P(('win', 'var')), parts along dimension 0
- var_grad_rows: float32 [480, 512], P(('win', 'var')), parts along dimension 0
- key_grad: float32 [1024, 512], P('win'), parts along dimension 0
- value_grad: float32 [1024, 512], P('win'), parts along dimension 0
There are 2 independent parts, one for each index of `win`. A program takes and returns all parts, laid end to end along the dimension named above; an argument that names none is the same for every part. Nothing has to cross between parts.
All inputs are finite; a program needn't handle non-finite values.
Results may differ from a plain program's by a relative error of at most 0.017.
Values may be sent and summed in bfloat16 or wider, within the bound.
A program may use at most 128 MiB of HBM per device.

v0:
```python
import jax
import jax.numpy as jnp
from jax import lax
from jax.sharding import PartitionSpec as P


def attend(tokens, bias_rows, latent_query, w_key, w_value, w_out, lat_rows, cotangent):
    var_count, patch_count, width = tokens.shape
    head_count, head_size = latent_query.shape
    score_scale = head_size ** (-0.5)
    flat_tokens = tokens.reshape(var_count * patch_count, width)
    key_rows = jnp.dot(flat_tokens, w_key, preferred_element_type=jnp.float32)
    key_heads = key_rows.reshape(var_count, patch_count, head_count, head_size)
    inverse_rms = lax.rsqrt(jnp.mean(key_heads * key_heads, axis=-1, keepdims=True) + 1e-06)
    normed = key_heads * inverse_rms
    scores = (
        jnp.einsum("vphe,he->phv", normed, latent_query, precision=lax.Precision.HIGHEST)
        * score_scale
        + bias_rows.T[None]
    )
    largest = jnp.max(scores, axis=-1, keepdims=True)
    raised = jnp.exp(scores - largest)
    weights = raised / jnp.sum(raised, axis=-1, keepdims=True)
    attn_rounded = weights.astype(jnp.bfloat16)
    mixed_rows = jnp.einsum(
        "phv,vpd->phd", attn_rounded, tokens, preferred_element_type=jnp.float32
    ).astype(jnp.bfloat16)
    value_heads = w_value.reshape(width, head_count, head_size)
    context = (
        jnp.einsum("phd,dhe->phe", mixed_rows, value_heads, preferred_element_type=jnp.float32)
        .astype(jnp.bfloat16)
        .reshape(patch_count, width)
    )
    output = (jnp.dot(context, w_out, preferred_element_type=jnp.float32) + lat_rows).astype(
        jnp.bfloat16
    )
    grad_context = jnp.dot(cotangent, w_out.T, preferred_element_type=jnp.float32).astype(
        jnp.bfloat16
    )
    grad_heads = grad_context.reshape(patch_count, head_count, head_size)
    value_grad = jnp.einsum(
        "phd,phe->dhe", mixed_rows, grad_heads, preferred_element_type=jnp.float32
    ).reshape(width, width)
    grad_mixed = jnp.einsum(
        "phe,dhe->phd", grad_heads, value_heads, preferred_element_type=jnp.float32
    ).astype(jnp.bfloat16)
    grad_attn = jnp.einsum("phd,vpd->phv", grad_mixed, tokens, preferred_element_type=jnp.float32)
    grad_scores = weights * (grad_attn - jnp.sum(weights * grad_attn, axis=-1, keepdims=True))
    grad_normed = (
        jnp.einsum("phv,he->vphe", grad_scores, latent_query, precision=lax.Precision.HIGHEST)
        * score_scale
    )
    grad_keys = (
        inverse_rms
        * (grad_normed - normed * jnp.mean(grad_normed * normed, axis=-1, keepdims=True))
    ).astype(jnp.bfloat16)
    grad_keys = grad_keys.reshape(var_count * patch_count, width)
    key_grad = jnp.einsum("nd,ne->de", flat_tokens, grad_keys, preferred_element_type=jnp.float32)
    through_keys = jnp.dot(grad_keys, w_key.T, preferred_element_type=jnp.float32).reshape(
        var_count, patch_count, width
    )
    through_values = jnp.einsum(
        "phv,phd->vpd", attn_rounded, grad_mixed, preferred_element_type=jnp.float32
    )
    token_grad = (through_values + through_keys).astype(jnp.bfloat16)
    return (output, token_grad, key_grad, value_grad)


def embed_tokens(patches, w_rows, emb_rows):
    summed = jnp.einsum("vpk,vkd->vpd", patches, w_rows, preferred_element_type=jnp.float32)
    return (summed + emb_rows[:, None, :]).astype(jnp.bfloat16)


def local(
    fields,
    var_ids,
    level_of,
    window_offset,
    w_embed,
    var_emb,
    w_key,
    w_value,
    w_out,
    latent_query,
    bias_table,
    lat_emb,
    d_aggregated,
):
    local_vars, local_rows, merged = fields.shape
    pixels = w_embed.shape[1]
    width = w_embed.shape[2]
    row_count = d_aggregated.shape[0]
    own_cols = d_aggregated.shape[1]
    level_count = bias_table.shape[0]
    all_cols = merged // pixels
    var_devices = lax.axis_size("var")
    patch_devices = lax.axis_size("patch")
    levels = jnp.take(level_of, var_ids, axis=0)
    one_hot = (levels[:, None] == jnp.arange(level_count, dtype=jnp.int32)[None, :]).astype(
        jnp.float32
    )
    bias_rows = jnp.dot(one_hot, bias_table, precision=lax.Precision.HIGHEST)
    lat_slice = lax.dynamic_slice_in_dim(lat_emb, window_offset[0], row_count, 0)
    lat_rows = lat_slice[:, None, :].reshape(row_count * own_cols, width)
    cotangent = d_aggregated.reshape(row_count * own_cols, width)
    row_start = lax.axis_index("var") * local_vars
    local_ids = lax.dynamic_slice_in_dim(var_ids, row_start, local_vars, 0)
    w_rows = jnp.take(w_embed, local_ids, axis=0)
    emb_rows = jnp.take(var_emb, local_ids, axis=0)
    patches = fields.reshape(local_vars, local_rows * all_cols, pixels)
    local_tokens = embed_tokens(patches, w_rows, emb_rows).reshape(
        local_vars, local_rows, all_cols * width
    )
    owned_tokens = lax.all_to_all(
        lax.all_to_all(local_tokens, "var", split_axis=2, concat_axis=0, tiled=True),
        "patch",
        split_axis=2,
        concat_axis=1,
        tiled=True,
    )
    output, token_grad, key_grad, value_grad = attend(
        owned_tokens, bias_rows, latent_query, w_key, w_value, w_out, lat_rows, cotangent
    )
    returned = lax.all_to_all(
        lax.all_to_all(token_grad, "var", split_axis=0, concat_axis=2, tiled=True),
        "patch",
        split_axis=1,
        concat_axis=2,
        tiled=True,
    )
    returned = returned.reshape(
        local_vars, local_rows, patch_devices, var_devices, own_cols * width
    )
    local_grad = returned.transpose(0, 1, 3, 2, 4).reshape(local_vars, local_rows * all_cols, width)
    embed_part = jnp.einsum("vpk,vpd->vkd", patches, local_grad, preferred_element_type=jnp.float32)
    var_part = jnp.sum(local_grad, axis=1, dtype=jnp.float32)
    embed_grad, var_grad = (
        lax.psum(embed_part.astype(jnp.bfloat16), "patch").astype(jnp.float32),
        lax.psum(var_part.astype(jnp.bfloat16), "patch").astype(jnp.float32),
    )
    key_grad, value_grad = lax.psum((key_grad, value_grad), ("var", "patch"))
    return (output.reshape(row_count, own_cols, width), embed_grad, var_grad, key_grad, value_grad)


def solution(mesh):
    in_specs = (
        P(("win", "var"), "patch", None),
        P(),
        P(),
        P("win"),
        P(),
        P(),
        P(),
        P(),
        P(),
        P(),
        P(),
        P(),
        P("win", ("var", "patch"), None),
    )
    out_specs = (
        P("win", ("var", "patch"), None),
        P(("win", "var"), None, None),
        P(("win", "var"), None),
        P("win", None),
        P("win", None),
    )
    return jax.shard_map(local, mesh=mesh, in_specs=in_specs, out_specs=out_specs, check_vma=False)
```

profile of v0, /device:TPU:1, one launch (start us, length us, event | category | flops | bytes accessed | tf_op | source)
XLA Modules:
  0.0 1303.5 jit_solution(16177951120995973303)
XLA Ops:
  25.4 9.9 reshape.98
  35.4 38.3 %copy.94 = bf16[30,2,32768]{0,1,2:T(2,128)(2,1)} copy(bf16[30,2,32768]{2,1,0:T(2,128)(2,1)} %reshape.98) | data formatting | bytes 7864320 | tf_op jit(solution)/shard_map/reshape | solution.py:111
  73.7 39.7 %reshape.143 = bf16[8,2,122880]{2,1,0:T(2,128)(2,1)} reshape(bf16[32768,2,30]{2,1,0:T(2,128)(2,1)} %bitcast.123) | data formatting | bytes 7864320
  113.4 56.1 %all_to_all.66 = bf16[8,2,122880]{2,1,0:T(2,128)(2,1)} all-to-all(bf16[8,2,122880]{2,1,0:T(2,128)(2,1)} %reshape.143), channel_id=1, replica_groups=mesh['var'=8,'patch'=8,'win'=2] {'var'}, dimensions={0} | all-to-all | bytes 7864320 | tf_op jit(solution)/shard_map/all_to_all | solution.py:115
  169.5 46.5 %reshape.144 = bf16[32768,2,30]{2,1,0:T(2,128)(2,1)} reshape(bf16[8,2,122880]{2,1,0:T(2,128)(2,1)} %all_to_all.66) | data formatting | bytes 7864320
  216.0 40.5 %copy.95 = bf16[30,2,8,4096]{3,1,0,2:T(2,128)(2,1)} copy(bf16[30,2,8,4096]{0,1,3,2:T(2,128)(2,1)} %bitcast.124) | data formatting | bytes 7864320 | tf_op jit(solution)/shard_map/all_to_all | solution.py:115
  256.6 14.9 %copy.96 = bf16[240,2,4096]{0,1,2:T(2,128)(2,1)} copy(bf16[240,2,4096]{2,1,0:T(2,128)(2,1)} %bitcast.132) | data formatting | bytes 7864320 | tf_op jit(solution)/shard_map/all_to_all | solution.py:115
  281.3 45.5 %all-to-all-done.1 = bf16[240,2,4096]{0,1,2:T(2,128)(2,1)} async-done(((bf16[240,2,4096]{0,1,2:T(2,128)(2,1)}), bf16[240,2,4096]{0,1,2:T(2,128)(2,1)}, u32[]{:S(2)}, u32[]{:S(2)}) %all-to-all-start.1) | async-done | bytes 3932192 | tf_op jit(solution)/shard_map/all_to_all | solution.py:114
  326.9 15.9 %copy.97 = bf16[240,2,8,512]{3,1,2,0:T(2,128)(2,1)} copy(bf16[240,2,8,512]{0,1,3,2:T(2,128)(2,1)} %bitcast.5) | data formatting | bytes 7864320 | tf_op jit(solution)/shard_map/all_to_all | solution.py:114
  342.7 9.1 reshape.136
  351.8 9.8 multiply_reduce_fusion
  361.8 11.1 copy.128
  379.6 33.2 %fusion.5 = f32[8,1,240,16]{2,1,3,0:T(1,128)S(1)} fusion(f32[8,64,1,1]{1,2,3,0:T(1,128)S(1)} %bitcast.140, f32[240,16,8,64]{3,1,2,0:T(8,128)S(1)} %broadcast_multiply_fusion), kind=kOutput, calls=%fused_computation.10 | convolution fusion | flops 23592960 | bytes 7989248 | tf_op jit(solution)/shard_map/vphe,he->phv/dot_general | solution.py:17
  416.8 15.7 %fusion.2 = f32[240,16,8]{1,2,0:T(8,128)S(1)} fusion(f32[8,64]{1,0:T(8,128)S(1)} %copy-done.15, f32[8,16,240]{1,0,2:T(8,128)S(1)} %copy.107, f32[240,16,8,64]{3,1,2,0:T(8,128)} %get-tuple-element.10, f32[240,16,8]{1,2,0:T(8,128)S(1)} %add_rsqrt_fusion), kind=kLoop, calls=%fused_computation.7 | loop fusion | flops 9799680 | bytes 8235008 | tf_op jit(solution)/shard_map/reduce_sum | solution.py:55
  432.5 17.5 %fusion.4 = bf16[240,16,8,64]{3,1,2,0:T(8,128)(2,1)} fusion(f32[240,16,8]{1,2,0:T(8,128)S(1)} %broadcast_multiply_fusion.1, f32[8,64]{1,0:T(8,128)S(1)} %copy-done.15, f32[8,16,240]{1,0,2:T(8,128)S(1)} %copy.107, f32[240,16,8]{1,2,0:T(8,128)S(1)} %add_rsqrt_fusion, f32[240,16,8,64]{3,1,2,0:T(8,128)} %get-tuple-element.10), kind=kLoop, calls=%fused_computation.9 | loop fusion | flops 13762560 | bytes 12167168 | tf_op jit(solution)/shard_map/convert_element_type | solution.py:56
  450.0 10.4 copy.108
  468.7 49.6 %all_to_all.67 = bf16[240,16,512]{2,1,0:T(8,128)(2,1)S(1)} all-to-all(bf16[240,16,512]{2,1,0:T(8,128)(2,1)S(1)} %copy.111), channel_id=1, replica_groups=mesh['var'=8,'patch'=8,'win'=2] {'var'}, dimensions={0} | all-to-all | bytes 7864320 | tf_op jit(solution)/shard_map/all_to_all | solution.py:125
  535.5 10.3 copy.117
  545.8 9.1 reshape.106
  554.9 11.2 reshape.107
  574.7 9.5 all-to-all-done.3
  601.4 21.2 %psum.29 = bf16[30,512]{1,0:T(8,128)(2,1)S(1)} all-reduce(bf16[30,512]{1,0:T(8,128)(2,1)S(1)} %bitcast_reduce_fusion.1), channel_id=1, replica_groups=mesh['var'=8,'patch'=8,'win'=2] {'patch'}, use_global_device_ids=true, to_apply=%region_7.8 | all-reduce | flops 15360 | bytes 61440 | tf_op jit(solution)/shard_map/psum | solution.py:139
  623.2 23.5 %all-reduce.4.cloned.1.call-done = bf16[30,16,512]{2,1,0:T(8,128)(2,1)} async-done(((bf16[30,16,512]{2,1,0:T(8,128)(2,1)}), bf16[30,16,512]{2,1,0:T(8,128)(2,1)}) %all-reduce.4.cloned.1.call-update) | async-done | bytes 491536 | tf_op jit(solution)/shard_map/psum | solution.py:138
  648.7 643.1 %all-reduce.6.cloned.1.call-done = (f32[512,512]{1,0:T(8,128)}, f32[512,512]{1,0:T(8,128)}) async-done(((f32[512,512]{1,0:T(8,128)}, f32[512,512]{1,0:T(8,128)}), (f32[512,512]{1,0:T(8,128)}, f32[512,512]{1,0:T(8,128)})) %all-reduce.6.cloned.1.call-update) | async-done | bytes 2097168 | tf_op jit(solution)/shard_map/psum | solution.py:141
  (91 shorter events, 96.6 us)
Async XLA Ops:
  7.2 271.2 %copy-start = (bf16[512,512]{1,0:T(8,128)(2,1)S(1)}, bf16[512,512]{1,0:T(8,128)(2,1)}, u32[]{:S(2)}) copy-start(bf16[512,512]{1,0:T(8,128)(2,1)} %param.21) | copy-start | bytes 1572868
  14.1 11.4 copy-start.10
  271.4 6.5 copy-start.5
  271.4 6.7 copy-start.12
  271.4 7.0 copy-start.16
  271.4 7.3 copy-start.17
  271.5 7.4 copy-start.1
  271.5 9.3 copy-start.18
  271.5 55.4 %all-to-all-start.1 = ((bf16[240,2,4096]{0,1,2:T(2,128)(2,1)}), bf16[240,2,4096]{0,1,2:T(2,128)(2,1)}, u32[]{:S(2)}, u32[]{:S(2)}) async-start(bf16[240,2,4096]{0,1,2:T(2,128)(2,1)} %copy.96), calls=%async_computation.1 | async-start | bytes 8388608 | tf_op jit(solution)/shard_map/all_to_all | solution.py:114
  278.8 64.0 %copy-start.13 = (bf16[16,8,64]{2,1,0:T(8,128)(2,1)}, bf16[16,8,64]{2,1,0:T(8,128)(2,1)S(1)}, u32[]{:S(2)}) copy-start(bf16[16,8,64]{2,1,0:T(8,128)(2,1)S(1)} %reshape.103) | copy-start | bytes 49156
  281.3 131.8 %copy-start.8 = (bf16[16,8,512]{2,0,1:T(8,128)(2,1)}, bf16[16,8,512]{2,0,1:T(8,128)(2,1)S(1)}, u32[]{:S(2)}) copy-start(bf16[16,8,512]{2,0,1:T(8,128)(2,1)S(1)} %fusion.13) | copy-start | bytes 393220
  372.8 6.8 copy-start.15
  379.6 33.5 %copy-start.2 = (bf16[240,8,2,512]{3,0,2,1:T(8,128)(2,1)S(1)}, bf16[240,8,2,512]{3,0,2,1:T(8,128)(2,1)}, u32[]{:S(2)}) copy-start(bf16[240,8,2,512]{3,0,2,1:T(8,128)(2,1)} %copy.128) | copy-start | bytes 11796484
  413.1 1.1 copy-start.6
  460.4 4.7 copy-start.7
  460.4 4.7 copy-start.9
  528.9 55.3 %all-to-all-start.3 = ((bf16[30,16,4096]{2,0,1:T(8,128)(2,1)}), bf16[30,16,4096]{2,0,1:T(8,128)(2,1)}, u32[]{:S(2)}, u32[]{:S(2)}) async-start(bf16[30,16,4096]{2,0,1:T(8,128)(2,1)} %reshape.142), calls=%async_computation.3 | async-start | bytes 8388608 | tf_op jit(solution)/shard_map/all_to_all | solution.py:124
  535.3 111.3 %all-reduce.4.cloned.1.call-start = ((), (), s32[]{:S(2)}) async-start(), calls=%async_computation.4 | async-start | bytes 983040 | tf_op jit(solution)/shard_map/psum | solution.py:138
  566.1 3.3 copy-start.4
  574.7 15.8 %copy-start.11 = (bf16[30,128,16]{1,2,0:T(8,128)(2,1)S(1)}, bf16[30,128,16]{1,2,0:T(8,128)(2,1)}, u32[]{:S(2)}) copy-start(bf16[30,128,16]{1,2,0:T(8,128)(2,1)} %copy-done.10) | copy-start | bytes 368644
  588.5 1.9 copy-start.3
  588.6 3.6 copy-start.14
  591.9 700.0 %all-reduce.6.cloned.1.call-start = ((), (), s32[]{:S(2)}) async-start(), calls=%async_computation.5 | async-start | bytes 4194304 | tf_op jit(solution)/shard_map/psum | solution.py:141
Sparse Core Ops, SparseCore 0:
  592.0 54.5 all-reduce.3
  649.8 641.9 all-reduce.5
where the time goes:
time: 1320 us; the launch traced here: 1300 us
  waiting for transfers between devices  722 us (55%)
  local copies, waits for them, and re-layouts  313 us (24%)
  blocking collectives  127 us (10%)
  matrix products  67.6 us (5%)
  other arithmetic  46 us (3%)
  between operations  15.3 us (1%)
  starting transfers between devices  13.4 us (1%)
    psum x1, waiting for transfers between devices, local(): key_grad, value_grad = lax.psum((key_grad, value_grad), ('var', 'patch'))  643 us
    unnamed x46, local copies, waits for them, and re-layouts  98.9 us
    all_to_all x1, blocking collectives, local(): lax.all_to_all(local_tokens, 'var', split_axis=2, concat_axis=0, tiled=True)  56.1 us
    all_to_all x2, local copies, waits for them, and re-layouts, local(): lax.all_to_all(local_tokens, 'var', split_axis=2, concat_axis=0, tiled=True)  55.4 us
    all_to_all x1, blocking collectives, local(): lax.all_to_all(token_grad, 'var', split_axis=0, concat_axis=2, tiled=True)  49.6 us
    reshape x2, local copies, waits for them, and re-layouts, local(): embed_tokens(patches, w_rows, emb_rows)  48.2 us
    all_to_all x1, waiting for transfers between devices, local(): lax.all_to_all(lax.all_to_all(local_tokens, 'var', split_axis=2, concat_a...  45.5 us
    dot_general x1, matrix products, attend(): jnp.einsum('vphe,he->phv', normed, latent_query, precision=lax.Precision....  33.2 us
  transfers between devices with their start and end apart: 4, of which 4 were waited for; matrix products, arithmetic and copies ran while one was open for 4% of the time, Pallas kernels for 0%

commit v1 on v0

v1 whole, which is shorter than its diff:
```python
import jax
import jax.numpy as jnp
from jax import lax
from jax.sharding import PartitionSpec as P


def local(
    fields,
    var_ids,
    level_of,
    window_offset,
    w_embed,
    var_emb,
    w_key,
    w_value,
    w_out,
    latent_query,
    bias_table,
    lat_emb,
    d_aggregated,
):
    f32, bf16 = jnp.float32, jnp.bfloat16
    nv, nr, merged = fields.shape
    pix, width = w_embed.shape[1:]
    heads, dh = latent_query.shape
    rows = d_aggregated.shape[0]
    cols = merged // pix
    npatch = nr * cols
    nvar, npat = lax.axis_size("var"), lax.axis_size("patch")
    i, j = lax.axis_index("var"), lax.axis_index("patch")
    ids = lax.dynamic_slice_in_dim(var_ids, i * nv, nv, 0)
    bias = jnp.take(bias_table, jnp.take(level_of, ids, axis=0), axis=0)
    wa = jnp.concatenate(
        [jnp.take(w_embed, ids, axis=0), jnp.take(var_emb, ids, axis=0)[:, None]], axis=1
    )
    wkv = jnp.concatenate([w_key, w_value], axis=1)
    we = jnp.einsum("vkd,de->vke", wa, wkv, preferred_element_type=f32).astype(bf16)
    f = fields.reshape(nv, npatch, pix).transpose(0, 2, 1)
    f = jnp.concatenate([f, jnp.ones((nv, 1, npatch), bf16)], axis=1)
    gc = jnp.dot(d_aggregated[:, 0], w_out.T, preferred_element_type=f32).astype(bf16)
    gc = lax.all_to_all(gc.reshape(npat, nr, width), "patch", 0, 0, tiled=True)
    gc = lax.all_gather(gc, "var")
    gc = gc.transpose(2, 0, 1, 3).reshape(npatch, width)
    gct = gc.astype(f32).T.reshape(heads, dh, npatch)
    kv = jnp.einsum("vke,vkp->vep", we, f, preferred_element_type=f32)
    keys = kv[:, :width].reshape(nv, heads, dh, npatch)
    vals = kv[:, width:].reshape(nv, heads, dh, npatch)
    inv = lax.rsqrt(jnp.mean(keys * keys, axis=2) + 1e-6)
    scale = dh**-0.5
    s0 = scale * inv * jnp.sum(keys * latent_query[None, :, :, None], axis=2)
    s = s0 + bias[:, :, None]
    ga = jnp.sum(vals * gct[None], axis=2)
    m = jnp.max(s, axis=0)
    e = jnp.exp(s - m)
    l = jnp.sum(e, axis=0)
    r = jnp.sum(e * ga, axis=0)
    ctx = jnp.sum(e[:, :, None] * vals, axis=0)
    stats = lax.all_gather(jnp.stack([m, l, r]), "var")
    mall = jnp.max(stats[:, 0], axis=0)
    fac = jnp.exp(stats[:, 0] - mall)
    lall = jnp.sum(fac * stats[:, 1], axis=0)
    rall = jnp.sum(fac * stats[:, 2], axis=0) / lall
    own = jnp.exp(m - mall) / lall
    ctx = ctx * own[:, None]
    ctx = ctx.reshape(width, nr, nvar, npat).transpose(2, 1, 3, 0)
    ctx = lax.psum_scatter(ctx, "var", scatter_dimension=0)
    ctx = ctx.reshape(nr, npat, width).astype(bf16)
    row0 = window_offset[0] + j * nr
    lat = lax.dynamic_slice_in_dim(lat_emb, row0, nr, 0).astype(f32)
    out = jnp.einsum("rpd,de->rpe", ctx, w_out, preferred_element_type=f32) + lat[:, None]
    out = lax.all_to_all(out.astype(bf16), "patch", 1, 0, tiled=True)
    out = out.reshape(rows, 1, width)
    attn = e * own
    gs = attn * (ga - rall)
    ca = scale * inv * gs
    cb = -inv * inv * gs * s0 / dh
    gk = ca[:, :, None] * latent_query[None, :, :, None] + cb[:, :, None] * keys
    ag = attn[:, :, None] * gct[None]
    g = jnp.concatenate(
        [gk.reshape(nv, width, npatch), ag.reshape(nv, width, npatch)], axis=1
    ).astype(bf16)
    fg = jnp.einsum("vkp,vep->vke", f, g, preferred_element_type=f32).astype(bf16)
    eg = jnp.einsum("vke,de->vkd", fg, wkv, preferred_element_type=f32).astype(bf16)
    kvg = jnp.einsum("vkd,vke->de", wa, fg, preferred_element_type=f32)
    eg = lax.psum(eg, "patch").astype(f32)
    kvg = lax.psum(kvg, ("var", "patch"))
    return out, eg[:, :pix], eg[:, pix], kvg[:, :width], kvg[:, width:]


def solution(mesh):
    split = P(("win", "var"), "patch", None)
    column = P("win", ("var", "patch"), None)
    in_specs = (split, P(), P(), P("win")) + (P(),) * 8 + (column,)
    out_specs = (
        column,
        P(("win", "var"), None, None),
        P(("win", "var"), None),
        P("win", None),
        P("win", None),
    )
    return jax.shard_map(local, mesh=mesh, in_specs=in_specs, out_specs=out_specs, check_vma=False)
```

time: 1320 us -> 835 us (0.63); the launches traced: 1300 us -> 835 us
  local copies, waits for them, and re-layouts: 313 us -> 18.6 us
  waiting for transfers between devices: 722 us -> 636 us
  matrix products: 67.6 us -> 18.9 us
  other arithmetic: 46 us -> 14.8 us
    unnamed x46 -> x24, local copies, waits for them, and re-layouts: 98.9 us -> 5.58 us
    all_to_all x6 -> x1, local copies, waits for them, and re-layouts: 86.2 us -> 0.62 us  [local(): out = lax.all_to_all(out.astype(bf16), 'patch', 1, 0, tiled=True)]
    all_to_all x2 -> x1, blocking collectives: 106 us -> 28.5 us  [local(): out = lax.all_to_all(out.astype(bf16), 'patch', 1, 0, tiled=True)]
    reshape x8 -> x2, local copies, waits for them, and re-layouts: 70.6 us -> 1.17 us  [the longest x1 0.64 us: local(): gc = lax.all_to_all(gc.reshape(npat, nr, width), 'patch', 0, 0, tiled=True)]
    all_gather x0 -> x2, blocking collectives: none -> 57.6 us  [the longest x1 29.3 us: local(): gc = lax.all_gather(gc, 'var')]
    all_to_all x2 -> x1, waiting for transfers between devices: 55.1 us -> 0.01 us  [local(): gc = lax.all_to_all(gc.reshape(npat, nr, width), 'patch', 0, 0, tiled=True)]
    dot_general x15 -> x6, matrix products: 67.6 us -> 18.9 us  [the longest x1 7.32 us: local(): kv = jnp.einsum('vke,vkp->vep', we, f, preferred_element_type=f32)]
    unnamed x0 -> x1, blocking collectives: none -> 39.1 us
  transfers between devices with their start and end apart: 4 -> 3, of which waited for: 4 -> 1; matrix products, arithmetic and copies ran while one was open for 4% -> 3% of each run, Pallas kernels for 0% -> 0%
where the time goes in v1:
time: 835 us
  waiting for transfers between devices  636 us (76%)
  blocking collectives  125 us (15%)
  matrix products  18.9 us (2%)
  local copies, waits for them, and re-layouts  18.6 us (2%)
  between operations  15 us (2%)
  other arithmetic  14.8 us (2%)
    psum x1, waiting for transfers between devices, local(): kvg = lax.psum(kvg, ('var', 'patch'))  636 us
    unnamed x1, blocking collectives  39.1 us
    all_gather x1, blocking collectives, local(): gc = lax.all_gather(gc, 'var')  29.3 us
    all_to_all x1, blocking collectives, local(): out = lax.all_to_all(out.astype(bf16), 'patch', 1, 0, tiled=True)  28.5 us
    all_gather x1, blocking collectives, local(): stats = lax.all_gather(jnp.stack([m, l, r]), 'var')  28.2 us
  transfers between devices with their start and end apart: 3, of which 1 were waited for; matrix products, arithmetic and copies ran while one was open for 3% of the time, Pallas kernels for 0%

profile of v1, /device:TPU:1, one launch (start us, length us, event | category | flops | bytes accessed | tf_op | source)
XLA Modules:
  0.0 834.9 jit_solution(4453085088806843712)
XLA Ops:
  7.2 1.0 copy-done
  8.2 0.9 convolution_convert_fusion.2
  9.8 6.0 all-to-all-start
  15.8 0.8 compare_and_fusion.1
  16.5 1.6 gather_fusion.1
  18.2 2.7 gather_fusion
  21.1 1.2 copy.87
  24.3 7.3 fusion.11
  31.8 29.3 %all-gather = bf16[64,2,512]{2,1,0:T(2,128)(2,1)S(1)} all-gather(bf16[8,2,512]{2,1,0:T(2,128)(2,1)S(1)} %all-to-all-done), channel_id=2, replica_groups=mesh['var'=8,'patch'=8,'win'=2] {'var'}, dimensions={0}, use_global_device_ids=true | all-gather | bytes 147456 | tf_op jit(solution)/shard_map/all_gather | solution.py:42
  61.2 8.4 %multiply_reduce_fusion = (f32[30,8,128]{2,1,0:T(8,128)S(1)}, f32[30,8,128]{2,1,0:T(8,128)S(1)}, f32[30,8,128]{2,1,0:T(8,128)S(1)}) fusion(f32[8,64,128]{2,1,0:T(8,128)S(1)} %bitcast.99, f32[30,1024,128]{2,1,0:T(8,128)} %fusion.11, f32[8,64]{1,0:T(8,128)S(1)} %copy-done.6), kind=kLoop, calls=%fused_computation.16 | loop fusion | flops 11704320 | bytes 16361472 | tf_op jit(solution)/shard_map/reduce_sum | solution.py:52
  69.9 28.2 %all-gather.1 = f32[24,8,128]{2,1,0:T(8,128)S(1)} all-gather(f32[3,8,128]{2,1,0:T(8,128)S(1)} %pad_maximum_fusion.4), channel_id=3, replica_groups=mesh['var'=8,'patch'=8,'win'=2] {'var'}, dimensions={0}, use_global_device_ids=true | all-gather | bytes 110592 | tf_op jit(solution)/shard_map/all_gather | solution.py:58
  98.3 1.0 fusion.4
  99.3 3.0 fusion.6
  102.3 4.4 fusion.8
  106.7 1.1 copy-done.9
  107.8 1.7 convolution_convert_fusion.1
  109.6 3.7 convolution_bitcast_fusion
  116.0 39.1 %all-reduce.9 = bf16[8,2,8,512]{3,2,0,1:T(8,128)(2,1)S(1)} all-reduce(f32[8,2,8,512]{3,2,0,1:T(8,128)S(1)} %multiply_bitcast_fusion), channel_id=4, replica_groups=mesh['var'=8,'patch'=8,'win'=2] {'var'}, use_global_device_ids=true, to_apply=%region_9.10.clone | all-reduce | flops 65536 | bytes 393216
  155.1 0.8 fusion.13
  156.0 28.5 %all_to_all.23 = bf16[2,8,512]{2,0,1:T(2,128)(2,1)S(1)} all-to-all(bf16[2,8,512]{2,0,1:T(2,128)(2,1)S(1)} %copy.96), channel_id=1, replica_groups=mesh['var'=8,'patch'=8,'win'=2] {'patch'}, dimensions={1} | all-to-all | bytes 32768 | tf_op jit(solution)/shard_map/all_to_all | solution.py:71
  185.1 1.2 slice.50
  186.3 1.5 copy.99
  188.6 636.4 %all-reduce.8.cloned.1.call-done = f32[512,1024]{1,0:T(8,128)} async-done(((f32[512,1024]{1,0:T(8,128)}), f32[512,1024]{1,0:T(8,128)}) %all-reduce.8.cloned.1.call-update) | async-done | bytes 2097168 | tf_op jit(solution)/shard_map/psum | solution.py:86
  825.0 3.0 fusion.37
  (57 shorter events, 6.9 us)
Async XLA Ops:
  7.2 1.0 copy-start
  7.2 15.7 %copy-start.7 = (f32[38,8]{0,1:T(8,128)S(1)}, f32[38,8]{0,1:T(8,128)}, u32[]{:S(2)}) copy-start(f32[38,8]{0,1:T(8,128)} %param.23) | copy-start | bytes 3652
  7.2 15.8 %copy-start.1 = (s32[240]{0:T(256)S(1)}, s32[240]{0:T(256)}, u32[]{:S(2)}) copy-start(s32[240]{0:T(256)} %param.15) | copy-start | bytes 2884
  7.2 17.1 %copy-start.4 = (bf16[512,512]{1,0:T(8,128)(2,1)S(1)}, bf16[512,512]{1,0:T(8,128)(2,1)}, u32[]{:S(2)}) copy-start(bf16[512,512]{1,0:T(8,128)(2,1)} %param.20) | copy-start | bytes 1572868
  7.2 17.1 %copy-start.5 = (bf16[512,512]{1,0:T(8,128)(2,1)S(1)}, bf16[512,512]{1,0:T(8,128)(2,1)}, u32[]{:S(2)}) copy-start(bf16[512,512]{1,0:T(8,128)(2,1)} %param.19) | copy-start | bytes 1572868
  9.8 22.0 %all-to-all-start = ((bf16[8,2,512]{2,1,0:T(2,128)(2,1)}), bf16[8,2,512]{2,1,0:T(2,128)(2,1)S(1)}, u32[]{:S(2)}, u32[]{:S(2)}) async-start(bf16[8,2,512]{2,1,0:T(2,128)(2,1)} %reshape.162), calls=%async_computation | async-start | bytes 32768 | tf_op jit(solution)/shard_map/all_to_all | solution.py:41
  15.8 169.3 %all-reduce.6.cloned.1.call-start = ((), (), s32[]{:S(2)}) async-start(), calls=%async_computation.2 | async-start | bytes 1114112 | tf_op jit(solution)/shard_map/psum | solution.py:85
  24.3 7.4 copy-start.6
  61.2 38.1 %copy-start.2 = (f32[30,1024,128]{2,1,0:T(8,128)S(1)}, f32[30,1024,128]{2,1,0:T(8,128)}, u32[]{:S(2)}) copy-start(f32[30,1024,128]{2,1,0:T(8,128)} %fusion.11) | copy-start | bytes 47185924
  106.7 1.1 copy-start.9
  109.5 4.5 copy-start.8
  109.5 715.5 %all-reduce.8.cloned.1.call-start = ((), (), s32[]{:S(2)}) async-start(), calls=%async_computation.3 | async-start | bytes 4194304 | tf_op jit(solution)/shard_map/psum | solution.py:86
  185.1 2.8 copy-start.3
Sparse Core Ops, SparseCore 0:
  109.6 71.7 all-reduce.5
  183.9 641.0 all-reduce.7

commit v2 on v1

v2 whole, which is shorter than its diff:
```python
import jax
import jax.numpy as jnp
from jax import lax
from jax.experimental import pallas as pl
from jax.experimental.pallas import tpu as pltpu
from jax.sharding import PartitionSpec as P

f32, bf16, i32 = jnp.float32, jnp.bfloat16, jnp.int32
NV, VL, PIX, D, H, DH, NP = 30, 15, 16, 512, 8, 64, 128
GR = 256
NN = (((1,), (0,)), ((), ()))
NT = (((1,), (1,)), ((), ()))


def iota(shape, dim):
    return lax.broadcasted_iota(i32, shape, dim)


def dot(a, b, dims=NN):
    return lax.dot_general(a, b, dims, preferred_element_type=f32)


def split(x):
    hi = x.astype(bf16)
    return hi, (x - hi.astype(f32)).astype(bf16)


def var_of(row):
    return jnp.where(row < VL * PIX, row >> 4, row - VL * PIX)


def kernel(
    ids_s, lvl_s, off_s, bias_s,
    fields_h, we_h, ve_h, wk_h, wv_h, wo_h, q_v, lat_v, d_h,
    agg_o, eg_o, kv_o,
    fld, wem, vem, wk, wv, wo, lsem,
    x_buf, x_ss, x_rs,
    g_snd, g_buf, g_ss, g_rs,
    st_buf, st_ss, st_rs,
    c_snd, c_buf, c_ss, c_rs,
    a_snd, a_buf, a_ss, a_rs,
    kvb, rk1, rk2, rk3, s1, s2, fink,
    egb, re1, re2, e1, fine,
    k_ss, k_rs, e_ss, e_rs,
    wa, wat, wek, wev, wekt, wevt, ff, fb, bi, ss, sn, ga, gc, at, ca, cb, eb, fg, ctxt,
):
    i, j = lax.axis_index("var"), lax.axis_index("patch")
    z, xh = i // 2, i % 2
    y, c = j // 2, j % 2
    q_me = y * 2 + xh

    def remote(src, dst, ssem, rsem, **dev):
        return pltpu.make_async_remote_copy(
            src_ref=src,
            dst_ref=dst,
            send_sem=ssem,
            recv_sem=rsem,
            device_id=dev,
            device_id_type=pl.DeviceIdType.MESH,
        )

    local = [
        pltpu.make_async_copy(src, dst, lsem.at[n])
        for n, (src, dst) in enumerate(
            [
                (fields_h, fld),
                (we_h, wem),
                (ve_h, vem.at[pl.ds(0, 240)]),
                (wk_h, wk),
                (wv_h, wv),
                (wo_h, wo),
                (d_h, x_buf.at[i]),
            ]
        )
    ]
    for cp in local:
        cp.start()

    barrier = pltpu.get_barrier_semaphore()
    peers = [dict(var=(i + t) % 8) for t in range(1, 8)]
    peers += [dict(patch=(j + t) % 8) for t in range(1, 8)]
    peers += [dict(var=z * 2 + 1 - xh, patch=((y + t) % 4) * 2 + c) for t in range(1, 4)]
    for dev in peers:
        pl.semaphore_signal(barrier, inc=1, device_id=dev, device_id_type=pl.DeviceIdType.MESH)
    pl.semaphore_wait(barrier, len(peers))

    xs = [remote(d_h, x_buf.at[i], x_ss.at[t - 1], x_rs.at[t - 1], var=(i + t) % 8) for t in range(1, 8)]
    for cp in xs:
        cp.start()

    def bias_step(v, _):
        lvl = lvl_s[ids_s[i * NV + v]]
        slot = v + v // VL
        for h in range(H):
            bi[h, pl.ds(slot, 1), :] = jnp.full((1, NP), bias_s[lvl, h], f32)
        return 0

    lax.fori_loop(0, NV, bias_step, 0)

    local[0].wait()
    lane_col = iota((8, NP), 1) >> 4
    own = lane_col == iota((8, NP), 0)
    pick = ((iota((PIX, NP), 1) & 15) == iota((PIX, NP), 0)).astype(bf16)
    for g in range(2):
        parts = []
        for v in range(VL):
            row = fld[g * VL + v].astype(f32)
            for b in range(8):
                for r in range(2):
                    piece = jnp.broadcast_to(row[r : r + 1, b * 128 : (b + 1) * 128], (8, 128))
                    parts.append(jnp.where(own, piece, 0.0))
        spread = jnp.concatenate(parts, axis=0).astype(bf16)
        ft = dot(pick, spread, NT)
        for v in range(VL):
            ff[g, v * PIX : (v + 1) * PIX, :] = ft[:, v * NP : (v + 1) * NP]
        ff[g, VL * PIX :, :] = jnp.where(iota((16, NP), 0) < VL, 1.0, 0.0)
        fb[g] = ff[g].astype(bf16)

    local[1].wait()

    def gather_step(v, _):
        g = v // VL
        row = pl.multiple_of(g * GR + (v - g * VL) * PIX, PIX)
        wa[pl.ds(row, PIX), :] = wem[ids_s[i * NV + v]]
        return 0

    lax.fori_loop(0, NV, gather_step, 0)
    vem[240:, :] = jnp.zeros((16, D), bf16)
    local[2].wait()
    for g in range(2):
        want = jnp.full((16, 256), -1, i32)
        for v in range(VL):
            want = jnp.where(iota((16, 256), 0) == v, ids_s[i * NV + g * VL + v], want)
        hot = jnp.where(want == iota((16, 256), 1), 1.0, 0.0).astype(bf16)
        wa[g * GR + VL * PIX : (g + 1) * GR, :] = dot(hot, vem[...]).astype(bf16)
    local[3].wait()
    local[4].wait()
    wat[...] = wa[...].T
    wek[...] = dot(wa[...], wk[...]).astype(bf16)
    wev[...] = dot(wa[...], wv[...]).astype(bf16)
    for g in range(2):
        wekt[g] = wek[g * GR : (g + 1) * GR, :].T
        wevt[g] = wev[g * GR : (g + 1) * GR, :].T

    local[5].wait()
    local[6].wait()
    for cp in xs:
        cp.wait()
    gx = dot(x_buf[...].reshape(NP, D), wo[...], NT).astype(bf16)
    o = iota((NP, NP), 0)
    src = ((o >> 1) & 7) * 16 + (o >> 4) * 2 + (o & 1)
    perm = jnp.where(src == iota((NP, NP), 1), 1.0, 0.0).astype(bf16)
    gs_rows = dot(perm, gx).astype(bf16)
    g_snd[...] = gs_rows.reshape(8, 16, D)
    gsends = []
    for t in range(1, 8):
        peer = (j + t) % 8
        gsends.append(remote(g_snd.at[peer], g_buf.at[j], g_ss.at[t - 1], g_rs.at[t - 1], patch=peer))
    for cp in gsends:
        cp.start()
    g_buf[j] = g_snd[j]

    spread_q = jnp.where((iota((DH, D), 1) & 63) == iota((DH, D), 0), 1.0, 0.0)
    qall = jnp.dot(q_v[...], spread_q, precision=lax.Precision.HIGHEST, preferred_element_type=f32)
    qblk = jnp.where((iota((H, D), 1) >> 6) == iota((H, D), 0), qall, 0.0)
    qrow = jnp.sum(qblk, axis=0, keepdims=True)
    wq = dot(jnp.concatenate(split(qblk), axis=0), wk[...], NT)
    wq = wq[:H] + wq[H:]
    aq = dot(jnp.concatenate(split(wq), axis=0), wa[...], NT)
    aq = aq[:H] + aq[H:]
    lane_var = var_of(iota((16, GR), 1))
    member = lane_var == iota((16, GR), 0)
    sums = jnp.where(member, 1.0, 0.0).astype(bf16)
    for g in range(2):
        rows = [
            jnp.where(member, jnp.broadcast_to(aq[h : h + 1, g * GR : (g + 1) * GR], (16, GR)), 0.0)
            for h in range(H)
        ]
        hi, lo = split(jnp.concatenate(rows, axis=0))
        got = dot(hi, fb[g]) + dot(lo, fb[g])
        for h in range(H):
            sn[h, g * 16 : (g + 1) * 16, :] = got[h * 16 : (h + 1) * 16]

    heads = jnp.where((iota((16, D), 1) >> 6) == iota((16, D), 0), 1.0, 0.0).astype(bf16)
    tile_row = iota((16, NP), 0)
    for g in range(2):
        ones = ff[g, VL * PIX :, :]
        for t in range(8):
            cols = []
            for v in (2 * t, 2 * t + 1):
                top = []
                if v < VL:
                    if v > 0:
                        top.append(jnp.zeros((v * PIX, NP), bf16))
                    top.append(fb[g, v * PIX : (v + 1) * PIX, :])
                    if v < VL - 1:
                        top.append(jnp.zeros(((VL - 1 - v) * PIX, NP), bf16))
                else:
                    top.append(jnp.zeros((VL * PIX, NP), bf16))
                top.append(jnp.where(tile_row == v, ones, 0.0).astype(bf16))
                cols.append(jnp.concatenate(top, axis=0))
            keys = dot(wekt[g], jnp.concatenate(cols, axis=1))
            sq = dot(heads, (keys * keys).astype(bf16))
            ss[:, g * 16 + 2 * t, :] = sq[:H, :NP]
            ss[:, g * 16 + 2 * t + 1, :] = sq[:H, NP:]

    scale = DH**-0.5
    slot = iota((H, 32, NP), 1)
    real = (slot & 15) < VL
    inv = lax.rsqrt(ss[...] * (1.0 / DH) + 1e-6)
    s0 = scale * inv * sn[...]
    s = jnp.where(real, s0 + bi[...], -1e30)
    m = jnp.max(s, axis=1, keepdims=True)
    e = jnp.where(real, jnp.exp(s - m), 0.0)
    at[...] = e
    st_buf[i, 0] = m[:, 0, :]
    st_buf[i, 1] = jnp.sum(e, axis=1)
    sn[...] = s0
    ss[...] = inv

    for cp in gsends:
        cp.wait()
    o = iota((NP, NP), 0)
    src = (o & 7) * 16 + (o >> 4) * 2 + ((o >> 3) & 1)
    perm = jnp.where(src == iota((NP, NP), 1), 1.0, 0.0).astype(bf16)
    gcf = dot(perm, g_buf[...].reshape(NP, D))
    gc[...] = gcf.astype(bf16)
    gct = gcf.T
    top_half = iota((NP, NP), 0) < DH
    for pair in range(4):
        piece = gct[pair * 128 : (pair + 1) * 128]
        blocks = jnp.concatenate(
            [jnp.where(top_half, piece, 0.0), jnp.where(top_half, 0.0, piece)], axis=1
        ).astype(bf16)
        for g in range(2):
            prod = dot(wev[g * GR : (g + 1) * GR, pair * 128 : (pair + 1) * 128], blocks)
            fg_rows = ff[g]
            hi, lo = split(prod * jnp.concatenate([fg_rows, fg_rows], axis=1))
            got = dot(sums, hi) + dot(sums, lo)
            ga[2 * pair, g * 16 : (g + 1) * 16, :] = got[:, :NP]
            ga[2 * pair + 1, g * 16 : (g + 1) * 16, :] = got[:, NP:]
    st_buf[i, 2] = jnp.sum(at[...] * ga[...], axis=1)
    sts = [
        remote(st_buf.at[i], st_buf.at[i], st_ss.at[t - 1], st_rs.at[t - 1], var=(i + t) % 8)
        for t in range(1, 8)
    ]
    for cp in sts:
        cp.start()
    for cp in sts:
        cp.wait()
    mall = st_buf[0, 0]
    for n in range(1, 8):
        mall = jnp.maximum(mall, st_buf[n, 0])
    lall = jnp.zeros((H, NP), f32)
    rall = jnp.zeros((H, NP), f32)
    for n in range(8):
        fac = jnp.exp(st_buf[n, 0] - mall)
        lall = lall + fac * st_buf[n, 1]
        rall = rall + fac * st_buf[n, 2]
    rall = rall / lall
    mine = jnp.exp(st_buf[i, 0] - mall) / lall
    attn = at[...] * mine[:, None, :]
    inv = ss[...]
    gs = attn * (ga[...] - rall[:, None, :])
    at[...] = attn
    ca[...] = scale * inv * gs
    cb[...] = (-1.0 / DH) * inv * inv * gs * sn[...]

    def times_fields(ref, h, g):
        x = ref[h, g * 16 : (g + 1) * 16, :]
        parts = [jnp.broadcast_to(x[v : v + 1], (PIX, NP)) for v in range(VL)] + [x]
        return (jnp.concatenate(parts, axis=0) * ff[g]).astype(bf16)

    low = iota((NP, 128), 1) < DH
    lowg = iota((GR, 128), 1) < DH
    zero = jnp.zeros((), bf16)
    for pair in range(4):
        lanes = slice(pair * 128, (pair + 1) * 128)
        piece = gc[:, lanes].astype(f32)
        gd = jnp.concatenate([jnp.where(low, piece, 0.0), jnp.where(low, 0.0, piece)], axis=0)
        gd = gd.astype(bf16)
        for g in range(2):
            pieces = []
            for n in range(2):
                x = times_fields(at, 2 * pair + n, g)
                eb[2 * pair + n, g * GR : (g + 1) * GR, :] = x
                pieces.append(x)
            fg[g * GR : (g + 1) * GR, D + pair * 128 : D + (pair + 1) * 128] = dot(
                jnp.concatenate(pieces, axis=1), gd
            ).astype(bf16)
    kvb[D:, :] = dot(wat[...], fg[:, D:]).astype(bf16)

    same = var_of(iota((GR, GR), 0)) == var_of(iota((GR, GR), 1))
    for pair in range(4):
        lanes = slice(pair * 128, (pair + 1) * 128)
        qp = jnp.broadcast_to(qrow[:, lanes], (NP, 128))
        qd = jnp.concatenate([jnp.where(low, qp, 0.0), jnp.where(low, 0.0, qp)], axis=0).astype(bf16)
        for g in range(2):
            wp = wek[g * GR : (g + 1) * GR, lanes].astype(f32)
            wd = jnp.concatenate([jnp.where(lowg, wp, 0.0), jnp.where(lowg, 0.0, wp)], axis=0)
            wd = wd.astype(bf16)
            af, ms = [], []
            for n in range(2):
                af.append(times_fields(ca, 2 * pair + n, g))
                mm = dot(times_fields(cb, 2 * pair + n, g), fb[g], NT)
                ms.append(jnp.where(same, mm, 0.0).astype(bf16))
            total = dot(jnp.concatenate(af, axis=1), qd) + dot(jnp.concatenate(ms, axis=1), wd)
            fg[g * GR : (g + 1) * GR, lanes] = total.astype(bf16)
    kvb[:D, :] = dot(wat[...], fg[:, :D]).astype(bf16)

    sib = y * 2 + 1 - c
    k1 = remote(kvb.at[pl.ds((1 - c) * D, D)], rk1, k_ss.at[0], k_rs.at[0], patch=sib)
    k1.start()
    for g in range(2):
        rows = slice(g * GR, (g + 1) * GR)
        egb[rows, :] = (dot(fg[rows, :D], wk[...], NT) + dot(fg[rows, D:], wv[...], NT)).astype(bf16)
    ex1 = remote(egb.at[pl.ds((1 - c) * GR, GR)], re1, e_ss.at[0], e_rs.at[0], patch=sib)
    ex1.start()

    for h in range(H):
        acc = dot(wevt[0, h * DH : (h + 1) * DH, :], eb[h, :GR, :])
        acc = acc + dot(wevt[1, h * DH : (h + 1) * DH, :], eb[h, GR:, :])
        ctxt[h * DH : (h + 1) * DH, :] = acc
    c_snd[...] = ctxt[...].T.astype(bf16).reshape(8, 16, D)
    cs = []
    for t in range(1, 8):
        peer = (i + t) % 8
        cs.append(remote(c_snd.at[peer], c_buf.at[i], c_ss.at[t - 1], c_rs.at[t - 1], var=peer))
    for cp in cs:
        cp.start()
    c_buf[i] = c_snd[i]

    k1.wait()
    s1[...] = (kvb[pl.ds(c * D, D), :].astype(f32) + rk1[...].astype(f32)).astype(bf16)
    k2 = []
    for t in range(1, 4):
        peer = (z + t) % 4
        k2.append(
            remote(s1.at[pl.ds(peer * 128, 128)], rk2.at[t - 1], k_ss.at[t], k_rs.at[t], var=peer * 2 + xh)
        )
    for cp in k2:
        cp.start()
    ex1.wait()
    e1[...] = (egb[pl.ds(c * GR, GR), :].astype(f32) + re1[...].astype(f32)).astype(bf16)
    ex2 = []
    for t in range(1, 4):
        peer = (y + t) % 4
        ex2.append(
            remote(e1.at[pl.ds(peer * 64, 64)], re2.at[t - 1], e_ss.at[t], e_rs.at[t], patch=peer * 2 + c)
        )
    for cp in ex2:
        cp.start()

    for cp in cs:
        cp.wait()
    cx = c_buf[0].astype(f32)
    for n in range(1, 8):
        cx = cx + c_buf[n].astype(f32)
    row = off_s[0] + 2 * j + (iota((16, 180), 0) >> 3)
    hot = jnp.where(row == iota((16, 180), 1), 1.0, 0.0).astype(bf16)
    agg = (dot(cx.astype(bf16), wo[...]) + dot(hot, lat_v[...])).astype(bf16)
    dst = iota((NP, 16), 0)
    r = (dst & 15) - 2 * j
    take = ((r >= 0) & (r < 2)) & (iota((NP, 16), 1) == r * 8 + (dst >> 4))
    a_snd[...] = dot(jnp.where(take, 1.0, 0.0).astype(bf16), agg).astype(bf16).reshape(8, 16, D)
    sends = []
    for t in range(1, 8):
        peer = (j + t) % 8
        sends.append(remote(a_snd.at[peer], a_buf.at[j], a_ss.at[t - 1], a_rs.at[t - 1], patch=peer))
    for cp in sends:
        cp.start()
    a_buf[j] = a_snd[j]

    for cp in k2:
        cp.wait()
    tot = s1[pl.ds(z * 128, 128), :].astype(f32)
    for n in range(3):
        tot = tot + rk2[n].astype(f32)
    s2[...] = tot.astype(bf16)
    k3 = []
    for t in range(1, 8):
        q = (q_me + t) % 8
        k3.append(
            remote(
                s2.at[pl.ds(q * 16, 16)], rk3.at[t - 1], k_ss.at[3 + t], k_rs.at[3 + t],
                var=z * 2 + q % 2, patch=(q // 2) * 2 + c,
            )
        )
    for cp in k3:
        cp.start()
    for cp in ex2:
        cp.wait()
    tot = e1[pl.ds(y * 64, 64), :].astype(f32)
    for n in range(3):
        tot = tot + re2[n].astype(f32)
    erow = c * GR + y * 64
    fine[pl.ds(erow, 64), :] = tot.astype(bf16)
    ex3 = []
    for t in range(1, 4):
        peer = (y + t) % 4
        own_rows = fine.at[pl.ds(erow, 64)]
        ex3.append(remote(own_rows, own_rows, e_ss.at[3 + t], e_rs.at[3 + t], patch=peer * 2 + c))
    for cp in ex3:
        cp.start()
    for cp in k3:
        cp.wait()
    tot = s2[pl.ds(q_me * 16, 16), :].astype(f32)
    for n in range(7):
        tot = tot + rk3[n].astype(f32)
    krow = c * D + z * 128
    own_rows = fink.at[pl.ds(krow + q_me * 16, 16)]
    fink[pl.ds(krow + q_me * 16, 16), :] = tot.astype(bf16)
    k4 = []
    for t in range(1, 8):
        q = (q_me + t) % 8
        k4.append(
            remote(
                own_rows, own_rows, k_ss.at[10 + t], k_rs.at[10 + t],
                var=z * 2 + q % 2, patch=(q // 2) * 2 + c,
            )
        )
    for cp in k4:
        cp.start()
    for cp in ex3:
        cp.wait()
    half = fine.at[pl.ds(c * GR, GR)]
    ex4 = remote(half, half, e_ss.at[7], e_rs.at[7], patch=sib)
    ex4.start()
    for cp in k4:
        cp.wait()
    k5 = []
    for t in range(1, 4):
        peer = (z + t) % 4
        part = fink.at[pl.ds(krow, 128)]
        k5.append(remote(part, part, k_ss.at[17 + t], k_rs.at[17 + t], var=peer * 2 + xh))
    for cp in k5:
        cp.start()

    for cp in sends:
        cp.wait()
    acc = a_buf[0].astype(f32)
    for n in range(1, 8):
        acc = acc + a_buf[n].astype(f32)
    a_snd[0] = acc.astype(bf16)
    outs = [pltpu.make_async_copy(a_snd.at[0], agg_o, lsem.at[7])]
    outs[0].start()
    ex4.wait()
    outs.append(pltpu.make_async_copy(fine, eg_o, lsem.at[8]))
    outs[1].start()
    for cp in k5:
        cp.wait()
    half = fink.at[pl.ds(c * D, D)]
    k6 = remote(half, half, k_ss.at[21], k_rs.at[21], patch=sib)
    k6.start()
    k6.wait()
    outs.append(pltpu.make_async_copy(fink, kv_o, lsem.at[9]))
    outs[2].start()
    for cp in outs:
        cp.wait()


def local(fields, var_ids, level_of, window_offset, w_embed, var_emb, w_key, w_value, w_out,
          latent_query, bias_table, lat_emb, d_aggregated):
    smem = pl.BlockSpec(memory_space=pltpu.SMEM)
    vmem = pl.BlockSpec(memory_space=pltpu.VMEM)
    hbm = pl.BlockSpec(memory_space=pl.ANY)
    dma = pltpu.SemaphoreType.DMA

    def v(*shape, dtype=bf16):
        return pltpu.VMEM(shape, dtype)

    scratch = [
        v(NV, 2, 1024), v(240, PIX, D), v(256, D), v(D, D), v(D, D), v(D, D), dma((10,)),
        v(8, 16, D), dma((7,)), dma((7,)),
        v(8, 16, D), v(8, 16, D), dma((7,)), dma((7,)),
        v(8, 3, H, NP, dtype=f32), dma((7,)), dma((7,)),
        v(8, 16, D), v(8, 16, D), dma((7,)), dma((7,)),
        v(8, 16, D), v(8, 16, D), dma((7,)), dma((7,)),
        v(2 * D, D), v(D, D), v(3, 128, D), v(7, 16, D), v(D, D), v(128, D), v(2 * D, D),
        v(D, D), v(GR, D), v(3, 64, D), v(GR, D), v(D, D),
        dma((22,)), dma((22,)), dma((8,)), dma((8,)),
        v(D, D), v(D, D), v(D, D), v(D, D), v(2, D, GR), v(2, D, GR),
        v(2, GR, NP, dtype=f32), v(2, GR, NP),
    ]
    scratch += [v(H, 32, NP, dtype=f32)] * 4 + [v(NP, D)] + [v(H, 32, NP, dtype=f32)] * 3
    scratch += [v(H, D, NP), v(D, 2 * D), v(D, NP, dtype=f32)]
    agg, eg, kv = pl.pallas_call(
        kernel,
        out_shape=[
            jax.ShapeDtypeStruct((16, D), bf16),
            jax.ShapeDtypeStruct((D, D), bf16),
            jax.ShapeDtypeStruct((2 * D, D), bf16),
        ],
        in_specs=[smem] * 4 + [hbm] * 6 + [vmem] * 2 + [hbm],
        out_specs=[hbm] * 3,
        scratch_shapes=scratch,
        compiler_params=pltpu.CompilerParams(
            collective_id=0, has_side_effects=True, vmem_limit_bytes=48 * 1024 * 1024
        ),
    )(
        var_ids, level_of, window_offset, bias_table,
        fields, w_embed, var_emb, w_key, w_value, w_out, latent_query, lat_emb,
        d_aggregated.reshape(16, D),
    )
    eg = eg.reshape(2, GR, D)
    embed = eg[:, : VL * PIX].astype(f32).reshape(NV, PIX, D)
    var = eg[:, VL * PIX : GR - 1].astype(f32).reshape(NV, D)
    kv = kv.astype(f32)
    return agg.reshape(16, 1, D), embed, var, kv[:D], kv[D:]


def solution(mesh):
    split_rows = P(("win", "var"), "patch", None)
    column = P("win", ("var", "patch"), None)
    in_specs = (split_rows, P(), P(), P("win")) + (P(),) * 8 + (column,)
    out_specs = (
        column,
        P(("win", "var"), None, None),
        P(("win", "var"), None),
        P("win", None),
        P("win", None),
    )
    return jax.shard_map(local, mesh=mesh, in_specs=in_specs, out_specs=out_specs, check_vma=False)
```

time: 835 us -> 76 us (0.09)
  waiting for transfers between devices: 636 us -> 0 us
  blocking collectives: 125 us -> 0 us
  Pallas kernels: 0 us -> 60.9 us
  matrix products: 18.9 us -> 0 us
  other arithmetic: 14.8 us -> 1.07 us
  between operations: 15 us -> 1.31 us
    psum x2 -> x0, waiting for transfers between devices: 636 us -> none  [the longest x1 636 us: local(): kvg = lax.psum(kvg, ('var', 'patch'))]
    pallas_call x0 -> x1, Pallas kernels: none -> 60.9 us  [local(): pl.pallas_call(kernel, out_shape=[jax.ShapeDtypeStruct((16, D), bf16), ja...]
    all_gather x2 -> x0, blocking collectives: 57.6 us -> none  [the longest x1 29.3 us: local(): gc = lax.all_gather(gc, 'var')]
    unnamed x1 -> x0, blocking collectives: 39.1 us -> none
    all_to_all x1 -> x0, blocking collectives: 28.5 us -> none  [local(): out = lax.all_to_all(out.astype(bf16), 'patch', 1, 0, tiled=True)]
    dot_general x6 -> x0, matrix products: 18.9 us -> none  [the longest x1 7.32 us: local(): kv = jnp.einsum('vke,vkp->vep', we, f, preferred_element_type=f32)]
    reduce_sum x3 -> x0, other arithmetic: 8.51 us -> none  [the longest x1 8.38 us: local(): ga = jnp.sum(vals * gct[None], axis=2)]
  transfers between devices with their start and end apart: 3 -> 0, of which waited for: 1 -> 0; matrix products, arithmetic and copies ran while one was open for 3% -> 0% of each run, Pallas kernels for 0% -> 0%
where the time goes in v2:
time: 76 us; the launch traced here: 75.6 us
  Pallas kernels  60.9 us (80%)
  local copies, waits for them, and re-layouts  12.3 us (16%)
  between operations  1.31 us (2%)
  other arithmetic  1.07 us (1%)
    pallas_call x1, Pallas kernels, local(): pl.pallas_call(kernel, out_shape=[jax.ShapeDtypeStruct((16, D), bf16), ja...  60.9 us
    unnamed x22, local copies, waits for them, and re-layouts  10 us
    slice x1, local copies, waits for them, and re-layouts, local(): return (agg.reshape(16, 1, D), embed, var, kv[:D], kv[D:])  1.61 us

profile of v2, /device:TPU:1, one launch (start us, length us, event | category | flops | bytes accessed | tf_op | source)
XLA Modules:
  0.0 75.6 jit_solution(16446845656067572730)
XLA Ops:
  0.6 0.8 %copy.19.bias_s = f32[38,8]{1,0:T(8,128)S(1)} copy(f32[38,8]{0,1:T(8,128)} %param.23) | data formatting | bytes 2432 | tf_op args[10]
  2.1 0.0 copy-start
  2.1 1.0 %copy-done = bf16[512,512]{1,0:T(8,128)(2,1)S(1)} copy-done((bf16[512,512]{1,0:T(8,128)(2,1)S(1)}, bf16[512,512]{1,0:T(8,128)(2,1)}, u32[]{:S(2)}) %copy-start) | copy-done | bytes 524312
  3.1 0.0 copy-start.1
  3.1 1.0 %copy-done.1 = bf16[512,512]{1,0:T(8,128)(2,1)S(1)} copy-done((bf16[512,512]{1,0:T(8,128)(2,1)S(1)}, bf16[512,512]{1,0:T(8,128)(2,1)}, u32[]{:S(2)}) %copy-start.1) | copy-done | bytes 524312
  4.1 0.0 copy-start.2
  4.1 1.0 %copy-done.2 = bf16[512,512]{1,0:T(8,128)(2,1)S(1)} copy-done((bf16[512,512]{1,0:T(8,128)(2,1)S(1)}, bf16[512,512]{1,0:T(8,128)(2,1)}, u32[]{:S(2)}) %copy-start.2) | copy-done | bytes 524312
  5.2 0.0 copy-start.3
  5.2 0.9 %copy-done.3 = bf16[240,512]{1,0:T(8,128)(2,1)S(1)} copy-done((bf16[240,512]{1,0:T(8,128)(2,1)S(1)}, bf16[240,512]{1,0:T(8,128)(2,1)}, u32[]{:S(2)}) %copy-start.3) | copy-done | bytes 245784
  6.1 0.0 copy-start.4
  6.1 0.9 %copy-done.4 = bf16[180,512]{1,0:T(8,128)(2,1)S(1)} copy-done((bf16[180,512]{1,0:T(8,128)(2,1)S(1)}, bf16[180,512]{1,0:T(8,128)(2,1)}, u32[]{:S(2)}) %copy-start.4) | copy-done | bytes 184344
  7.1 0.0 copy-start.5
  7.1 0.9 %copy-done.5 = bf16[30,2,1024]{2,1,0:T(2,128)(2,1)S(1)} copy-done((bf16[30,2,1024]{2,1,0:T(2,128)(2,1)S(1)}, bf16[30,2,1024]{2,1,0:T(2,128)(2,1)}, u32[]{:S(2)}) %copy-start.5) | copy-done | bytes 122904
  8.0 0.0 copy-start.6
  8.0 0.7 copy-done.6
  8.7 0.0 copy-start.7
  8.7 0.7 copy-done.7
  9.4 0.7 copy-done.8
  10.0 0.7 copy-done.9
  10.7 60.9 %shard_map.164 = (bf16[16,512]{1,0:T(8,128)(2,1)S(1)}, bf16[512,512]{1,0:T(8,128)(2,1)S(1)}, bf16[1024,512]{1,0:T(8,128)(2,1)S(1)}) custom-call(s32[240]{0:T(256)S(1)} %copy-done.8, s32[240]{0:T(256)S(1)} %copy-done.9, s32[1]{0:T(128)S(6)} %copy.21.off_s, f32[38,8]{1,0:T(8,128)S(1)} %copy.19.bias_s, bf16[30,2,1024]{2,1,0:T(2,128)(2,1)S(1)} %copy-done.5, ...), custom_call_target="tpu_custom_call" | custom-call | tf_op jit(solution)/shard_map/pallas_call | solution.py:487
  71.6 1.6 %fusion = (f32[512,512]{1,0:T(8,128)}, f32[512,512]{1,0:T(8,128)}) fusion(bf16[1024,512]{1,0:T(8,128)(2,1)S(1)} %get-tuple-element.10), kind=kLoop, calls=%fused_computation.1 | loop fusion | bytes 4194304 | tf_op jit(solution)/shard_map/slice | solution.py:509
  73.2 1.1 %convert.2 = f32[30,16,512]{2,1,0:T(8,128)} convert(bf16[30,16,512]{2,1,0:T(8,128)(2,1)S(1)} %bitcast.9) | non-fusion elementwise | flops 245760 | bytes 1474560 | tf_op jit(solution)/shard_map/reshape | solution.py:506
  74.3 0.6 reshape.41
  75.0 0.6 copy.22
  (4 shorter events, 0.0 us)
Async XLA Ops:
  2.1 1.0 %copy-start = (bf16[512,512]{1,0:T(8,128)(2,1)S(1)}, bf16[512,512]{1,0:T(8,128)(2,1)}, u32[]{:S(2)}) copy-start(bf16[512,512]{1,0:T(8,128)(2,1)} %wk_h.1) | copy-start | bytes 1572868
  3.1 1.0 %copy-start.1 = (bf16[512,512]{1,0:T(8,128)(2,1)S(1)}, bf16[512,512]{1,0:T(8,128)(2,1)}, u32[]{:S(2)}) copy-start(bf16[512,512]{1,0:T(8,128)(2,1)} %wv_h.1) | copy-start | bytes 1572868
  4.1 1.0 %copy-start.2 = (bf16[512,512]{1,0:T(8,128)(2,1)S(1)}, bf16[512,512]{1,0:T(8,128)(2,1)}, u32[]{:S(2)}) copy-start(bf16[512,512]{1,0:T(8,128)(2,1)} %wo_h.1) | copy-start | bytes 1572868
  5.2 0.9 %copy-start.3 = (bf16[240,512]{1,0:T(8,128)(2,1)S(1)}, bf16[240,512]{1,0:T(8,128)(2,1)}, u32[]{:S(2)}) copy-start(bf16[240,512]{1,0:T(8,128)(2,1)} %ve_h.1) | copy-start | bytes 737284
  6.1 0.9 %copy-start.4 = (bf16[180,512]{1,0:T(8,128)(2,1)S(1)}, bf16[180,512]{1,0:T(8,128)(2,1)}, u32[]{:S(2)}) copy-start(bf16[180,512]{1,0:T(8,128)(2,1)} %lat_v.1) | copy-start | bytes 552964
  7.1 0.9 %copy-start.5 = (bf16[30,2,1024]{2,1,0:T(2,128)(2,1)S(1)}, bf16[30,2,1024]{2,1,0:T(2,128)(2,1)}, u32[]{:S(2)}) copy-start(bf16[30,2,1024]{2,1,0:T(2,128)(2,1)} %fields_h.1) | copy-start | bytes 368644
  8.0 0.7 copy-start.6
  8.7 0.7 copy-start.7
  9.4 0.7 copy-start.8
  10.0 0.7 copy-start.9

commit v3 on v2

--- a/solution.py
+++ b/solution.py
@@ -30,37 +30,53 @@
 
 
 def kernel(
-    ids_s, lvl_s, off_s, bias_s,
-    fields_h, we_h, ve_h, wk_h, wv_h, wo_h, q_v, lat_v, d_h,
-    agg_o, eg_o, kv_o,
-    fld, wem, vem, wk, wv, wo, lsem,
+    ids_h, lvl_h, off_h, bias_h,
+    fields_h, we_h, ve_h, wk_h, wv_h, wo_h, q_h, lat_h, d_h,
+    agg_o, eg_o, kg_o, vg_o,
+    ids_s, lvl_s, off_s, bias_s, q_v, lat_v, fld, wem, vem, wk, wv, wo, lsem,
     x_buf, x_ss, x_rs,
     g_snd, g_buf, g_ss, g_rs,
-    st_buf, st_ss, st_rs,
+    ml_buf, ml_ss, ml_rs,
+    r_buf, r_ss, r_rs,
     c_snd, c_buf, c_ss, c_rs,
     a_snd, a_buf, a_ss, a_rs,
-    kvb, rk1, rk2, rk3, s1, s2, fink,
+    kb, kr1, kr2, kr3, ks1, ks2, kfin,
+    vb, vr1, vr2, vr3, vs1, vs2, vfin,
     egb, re1, re2, e1, fine,
-    k_ss, k_rs, e_ss, e_rs,
+    k_ss, k_rs, v_ss, v_rs, e_ss, e_rs,
     wa, wat, wek, wev, wekt, wevt, ff, fb, bi, ss, sn, ga, gc, at, ca, cb, eb, fg, ctxt,
 ):
     i, j = lax.axis_index("var"), lax.axis_index("patch")
     z, xh = i // 2, i % 2
     y, c = j // 2, j % 2
-    q_me = y * 2 + xh
+    w_me = z * 4 + y
+
+    pending = []
+
+    class Tr:
+        def __init__(self, cp):
+            self.cp = cp
+
+        def start(self):
+            self.cp.start()
+            pending.append(self)
+
+        def wait(self):
+            self.cp.wait()
+            pending.remove(self)
 
     def remote(src, dst, ssem, rsem, **dev):
-        return pltpu.make_async_remote_copy(
+        return Tr(pltpu.make_async_remote_copy(
             src_ref=src,
             dst_ref=dst,
             send_sem=ssem,
             recv_sem=rsem,
             device_id=dev,
             device_id_type=pl.DeviceIdType.MESH,
-        )
+        ))
 
     local = [
-        pltpu.make_async_copy(src, dst, lsem.at[n])
+        Tr(pltpu.make_async_copy(src, dst, lsem.at[n]))
         for n, (src, dst) in enumerate(
             [
                 (fields_h, fld),
@@ -70,6 +86,12 @@
                 (wv_h, wv),
                 (wo_h, wo),
                 (d_h, x_buf.at[i]),
+                (ids_h, ids_s),
+                (lvl_h, lvl_s),
+                (off_h, off_s),
+                (bias_h, bias_s),
+                (q_h, q_v),
+                (lat_h, lat_v),
             ]
         )
     ]
@@ -79,7 +101,11 @@
     barrier = pltpu.get_barrier_semaphore()
     peers = [dict(var=(i + t) % 8) for t in range(1, 8)]
     peers += [dict(patch=(j + t) % 8) for t in range(1, 8)]
-    peers += [dict(var=z * 2 + 1 - xh, patch=((y + t) % 4) * 2 + c) for t in range(1, 4)]
+    peers += [
+        dict(var=((z + t) % 4) * 2 + xh, patch=((y + n) % 4) * 2 + c)
+        for t in range(1, 4)
+        for n in range(1, 4)
+    ]
     for dev in peers:
         pl.semaphore_signal(barrier, inc=1, device_id=dev, device_id_type=pl.DeviceIdType.MESH)
     pl.semaphore_wait(barrier, len(peers))
@@ -88,11 +114,13 @@
     for cp in xs:
         cp.start()
 
+    for n in range(7, 13):
+        local[n].wait()
     def bias_step(v, _):
         lvl = lvl_s[ids_s[i * NV + v]]
         slot = v + v // VL
         for h in range(H):
-            bi[h, pl.ds(slot, 1), :] = jnp.full((1, NP), bias_s[lvl, h], f32)
+            bi[h, pl.ds(slot, 1), :] = jnp.full((1, NP), bias_s[h, lvl], f32)
         return 0
 
     lax.fori_loop(0, NV, bias_step, 0)
@@ -213,8 +241,14 @@
     m = jnp.max(s, axis=1, keepdims=True)
     e = jnp.where(real, jnp.exp(s - m), 0.0)
     at[...] = e
-    st_buf[i, 0] = m[:, 0, :]
-    st_buf[i, 1] = jnp.sum(e, axis=1)
+    ml_buf[i, 0] = m[:, 0, :]
+    ml_buf[i, 1] = jnp.sum(e, axis=1)
+    mls = [
+        remote(ml_buf.at[i], ml_buf.at[i], ml_ss.at[t - 1], ml_rs.at[t - 1], var=(i + t) % 8)
+        for t in range(1, 8)
+    ]
+    for cp in mls:
+        cp.start()
     sn[...] = s0
     ss[...] = inv
 
@@ -239,37 +273,84 @@
             got = dot(sums, hi) + dot(sums, lo)
             ga[2 * pair, g * 16 : (g + 1) * 16, :] = got[:, :NP]
             ga[2 * pair + 1, g * 16 : (g + 1) * 16, :] = got[:, NP:]
-    st_buf[i, 2] = jnp.sum(at[...] * ga[...], axis=1)
-    sts = [
-        remote(st_buf.at[i], st_buf.at[i], st_ss.at[t - 1], st_rs.at[t - 1], var=(i + t) % 8)
+    r_buf[i] = jnp.sum(at[...] * ga[...], axis=1)
+    rss = [
+        remote(r_buf.at[i], r_buf.at[i], r_ss.at[t - 1], r_rs.at[t - 1], var=(i + t) % 8)
         for t in range(1, 8)
     ]
-    for cp in sts:
-        cp.start()
-    for cp in sts:
-        cp.wait()
-    mall = st_buf[0, 0]
+    for cp in rss:
+        cp.start()
+    for cp in mls:
+        cp.wait()
+    mall = ml_buf[0, 0]
     for n in range(1, 8):
-        mall = jnp.maximum(mall, st_buf[n, 0])
+        mall = jnp.maximum(mall, ml_buf[n, 0])
     lall = jnp.zeros((H, NP), f32)
-    rall = jnp.zeros((H, NP), f32)
     for n in range(8):
-        fac = jnp.exp(st_buf[n, 0] - mall)
-        lall = lall + fac * st_buf[n, 1]
-        rall = rall + fac * st_buf[n, 2]
-    rall = rall / lall
-    mine = jnp.exp(st_buf[i, 0] - mall) / lall
-    attn = at[...] * mine[:, None, :]
-    inv = ss[...]
-    gs = attn * (ga[...] - rall[:, None, :])
-    at[...] = attn
-    ca[...] = scale * inv * gs
-    cb[...] = (-1.0 / DH) * inv * inv * gs * sn[...]
+        lall = lall + jnp.exp(ml_buf[n, 0] - mall) * ml_buf[n, 1]
+    mine = jnp.exp(ml_buf[i, 0] - mall) / lall
+    at[...] = at[...] * mine[:, None, :]
 
     def times_fields(ref, h, g):
         x = ref[h, g * 16 : (g + 1) * 16, :]
         parts = [jnp.broadcast_to(x[v : v + 1], (PIX, NP)) for v in range(VL)] + [x]
         return (jnp.concatenate(parts, axis=0) * ff[g]).astype(bf16)
+
+    def put(buf, x):
+        buf[:D, :] = x[:, : D // 2]
+        buf[D:, :] = x[:, D // 2 :]
+
+    sib = y * 2 + 1 - c
+
+    def core_sum_start(buf, r1, s_sem, r_sem):
+        cp = remote(buf.at[pl.ds((1 - c) * D, D)], r1, s_sem.at[0], r_sem.at[0], patch=sib)
+        cp.start()
+        return cp
+
+    def at16(w):
+        return dict(var=(w // 4) * 2 + xh, patch=(w % 4) * 2 + c)
+
+    def core_sum_end(cp, buf, r1, s1, r2, s_sem, r_sem):
+        cp.wait()
+        s1[...] = (buf[pl.ds(c * D, D), :].astype(f32) + r1[...].astype(f32)).astype(bf16)
+        cps = []
+        for t in range(1, 16):
+            w = (w_me + t) % 16
+            cps.append(remote(s1.at[pl.ds(w * 32, 32)], r2.at[t - 1], s_sem.at[t], r_sem.at[t], **at16(w)))
+        for cp in cps:
+            cp.start()
+        return cps
+
+    def zy_sum_end(cps, s1, r2, s2, r3, s_sem, r_sem):
+        for cp in cps:
+            cp.wait()
+        tot = s1[pl.ds(w_me * 32, 32), :].astype(f32)
+        for n in range(15):
+            tot = tot + r2[n].astype(f32)
+        s2[...] = tot.astype(bf16)
+        cp = remote(s2, r3, s_sem.at[16], r_sem.at[16], var=z * 2 + 1 - xh)
+        cp.start()
+        return cp
+
+    def x_sum_end(cp, s2, r3, fin, s_sem, r_sem):
+        cp.wait()
+        row = c * D + w_me * 32
+        fin[pl.ds(row, 32), :] = (s2[...].astype(f32) + r3[...].astype(f32)).astype(bf16)
+        rows = fin.at[pl.ds(row, 32)]
+        cps = []
+        for t in range(1, 16):
+            cps.append(remote(rows, rows, s_sem.at[16 + t], r_sem.at[16 + t], **at16((w_me + t) % 16)))
+        for cp in cps:
+            cp.start()
+        return cps
+
+    def gather_end(cps, fin, s_sem, r_sem):
+        for cp in cps:
+            cp.wait()
+        half = fin.at[pl.ds(c * D, D)]
+        cp = remote(half, half, s_sem.at[32], r_sem.at[32], patch=sib)
+        cp.start()
+        return cp
 
     low = iota((NP, 128), 1) < DH
     lowg = iota((GR, 128), 1) < DH
@@ -288,7 +369,33 @@
             fg[g * GR : (g + 1) * GR, D + pair * 128 : D + (pair + 1) * 128] = dot(
                 jnp.concatenate(pieces, axis=1), gd
             ).astype(bf16)
-    kvb[D:, :] = dot(wat[...], fg[:, D:]).astype(bf16)
+    put(vb, dot(wat[...], fg[:, D:]).astype(bf16))
+    v1 = core_sum_start(vb, vr1, v_ss, v_rs)
+
+    for h in range(H):
+        acc = dot(wevt[0, h * DH : (h + 1) * DH, :], eb[h, :GR, :])
+        acc = acc + dot(wevt[1, h * DH : (h + 1) * DH, :], eb[h, GR:, :])
+        ctxt[h * DH : (h + 1) * DH, :] = acc
+    c_snd[...] = ctxt[...].T.astype(bf16).reshape(8, 16, D)
+    cs = []
+    for t in range(1, 8):
+        peer = (i + t) % 8
+        cs.append(remote(c_snd.at[peer], c_buf.at[i], c_ss.at[t - 1], c_rs.at[t - 1], var=peer))
+    v2 = core_sum_end(v1, vb, vr1, vs1, vr2, v_ss, v_rs)
+    for cp in cs:
+        cp.start()
+    c_buf[i] = c_snd[i]
+
+    for cp in rss:
+        cp.wait()
+    rall = jnp.zeros((H, NP), f32)
+    for n in range(8):
+        rall = rall + jnp.exp(ml_buf[n, 0] - mall) * r_buf[n]
+    rall = rall / lall
+    inv = ss[...]
+    gs = at[...] * (ga[...] - rall[:, None, :])
+    ca[...] = scale * inv * gs
+    cb[...] = (-1.0 / DH) * inv * inv * gs * sn[...]
 
     same = var_of(iota((GR, GR), 0)) == var_of(iota((GR, GR), 1))
     for pair in range(4):
@@ -306,40 +413,15 @@
                 ms.append(jnp.where(same, mm, 0.0).astype(bf16))
             total = dot(jnp.concatenate(af, axis=1), qd) + dot(jnp.concatenate(ms, axis=1), wd)
             fg[g * GR : (g + 1) * GR, lanes] = total.astype(bf16)
-    kvb[:D, :] = dot(wat[...], fg[:, :D]).astype(bf16)
-
-    sib = y * 2 + 1 - c
-    k1 = remote(kvb.at[pl.ds((1 - c) * D, D)], rk1, k_ss.at[0], k_rs.at[0], patch=sib)
-    k1.start()
+    put(kb, dot(wat[...], fg[:, :D]).astype(bf16))
+    k1 = core_sum_start(kb, kr1, k_ss, k_rs)
     for g in range(2):
         rows = slice(g * GR, (g + 1) * GR)
         egb[rows, :] = (dot(fg[rows, :D], wk[...], NT) + dot(fg[rows, D:], wv[...], NT)).astype(bf16)
     ex1 = remote(egb.at[pl.ds((1 - c) * GR, GR)], re1, e_ss.at[0], e_rs.at[0], patch=sib)
     ex1.start()
 
-    for h in range(H):
-        acc = dot(wevt[0, h * DH : (h + 1) * DH, :], eb[h, :GR, :])
-        acc = acc + dot(wevt[1, h * DH : (h + 1) * DH, :], eb[h, GR:, :])
-        ctxt[h * DH : (h + 1) * DH, :] = acc
-    c_snd[...] = ctxt[...].T.astype(bf16).reshape(8, 16, D)
-    cs = []
-    for t in range(1, 8):
-        peer = (i + t) % 8
-        cs.append(remote(c_snd.at[peer], c_buf.at[i], c_ss.at[t - 1], c_rs.at[t - 1], var=peer))
-    for cp in cs:
-        cp.start()
-    c_buf[i] = c_snd[i]
-
-    k1.wait()
-    s1[...] = (kvb[pl.ds(c * D, D), :].astype(f32) + rk1[...].astype(f32)).astype(bf16)
-    k2 = []
-    for t in range(1, 4):
-        peer = (z + t) % 4
-        k2.append(
-            remote(s1.at[pl.ds(peer * 128, 128)], rk2.at[t - 1], k_ss.at[t], k_rs.at[t], var=peer * 2 + xh)
-        )
-    for cp in k2:
-        cp.start()
+    k2 = core_sum_end(k1, kb, kr1, ks1, kr2, k_ss, k_rs)
     ex1.wait()
     e1[...] = (egb[pl.ds(c * GR, GR), :].astype(f32) + re1[...].astype(f32)).astype(bf16)
     ex2 = []
@@ -371,23 +453,7 @@
         cp.start()
     a_buf[j] = a_snd[j]
 
-    for cp in k2:
-        cp.wait()
-    tot = s1[pl.ds(z * 128, 128), :].astype(f32)
-    for n in range(3):
-        tot = tot + rk2[n].astype(f32)
-    s2[...] = tot.astype(bf16)
-    k3 = []
-    for t in range(1, 8):
-        q = (q_me + t) % 8
-        k3.append(
-            remote(
-                s2.at[pl.ds(q * 16, 16)], rk3.at[t - 1], k_ss.at[3 + t], k_rs.at[3 + t],
-                var=z * 2 + q % 2, patch=(q // 2) * 2 + c,
-            )
-        )
-    for cp in k3:
-        cp.start()
+    v3 = zy_sum_end(v2, vs1, vr2, vs2, vr3, v_ss, v_rs)
     for cp in ex2:
         cp.wait()
     tot = e1[pl.ds(y * 64, 64), :].astype(f32)
@@ -402,39 +468,14 @@
         ex3.append(remote(own_rows, own_rows, e_ss.at[3 + t], e_rs.at[3 + t], patch=peer * 2 + c))
     for cp in ex3:
         cp.start()
-    for cp in k3:
-        cp.wait()
-    tot = s2[pl.ds(q_me * 16, 16), :].astype(f32)
-    for n in range(7):
-        tot = tot + rk3[n].astype(f32)
-    krow = c * D + z * 128
-    own_rows = fink.at[pl.ds(krow + q_me * 16, 16)]
-    fink[pl.ds(krow + q_me * 16, 16), :] = tot.astype(bf16)
-    k4 = []
-    for t in range(1, 8):
-        q = (q_me + t) % 8
-        k4.append(
-            remote(
-                own_rows, own_rows, k_ss.at[10 + t], k_rs.at[10 + t],
-                var=z * 2 + q % 2, patch=(q // 2) * 2 + c,
-            )
-        )
-    for cp in k4:
-        cp.start()
+    v4 = x_sum_end(v3, vs2, vr3, vfin, v_ss, v_rs)
+    k3 = zy_sum_end(k2, ks1, kr2, ks2, kr3, k_ss, k_rs)
     for cp in ex3:
         cp.wait()
     half = fine.at[pl.ds(c * GR, GR)]
     ex4 = remote(half, half, e_ss.at[7], e_rs.at[7], patch=sib)
     ex4.start()
-    for cp in k4:
-        cp.wait()
-    k5 = []
-    for t in range(1, 4):
-        peer = (z + t) % 4
-        part = fink.at[pl.ds(krow, 128)]
-        k5.append(remote(part, part, k_ss.at[17 + t], k_rs.at[17 + t], var=peer * 2 + xh))
-    for cp in k5:
-        cp.start()
+    k4 = x_sum_end(k3, ks2, kr3, kfin, k_ss, k_rs)
 
     for cp in sends:
         cp.wait()
@@ -442,71 +483,111 @@
     for n in range(1, 8):
         acc = acc + a_buf[n].astype(f32)
     a_snd[0] = acc.astype(bf16)
-    outs = [pltpu.make_async_copy(a_snd.at[0], agg_o, lsem.at[7])]
+    outs = [pltpu.make_async_copy(a_snd.at[0], agg_o, lsem.at[13])]
     outs[0].start()
     ex4.wait()
-    outs.append(pltpu.make_async_copy(fine, eg_o, lsem.at[8]))
+    outs.append(pltpu.make_async_copy(fine, eg_o, lsem.at[14]))
     outs[1].start()
-    for cp in k5:
-        cp.wait()
-    half = fink.at[pl.ds(c * D, D)]
-    k6 = remote(half, half, k_ss.at[21], k_rs.at[21], patch=sib)
-    k6.start()
-    k6.wait()
-    outs.append(pltpu.make_async_copy(fink, kv_o, lsem.at[9]))
+    v5 = gather_end(v4, vfin, v_ss, v_rs)
+    v5.wait()
+    outs.append(pltpu.make_async_copy(vfin, vg_o, lsem.at[15]))
     outs[2].start()
+    k5 = gather_end(k4, kfin, k_ss, k_rs)
+    k5.wait()
+    outs.append(pltpu.make_async_copy(kfin, kg_o, lsem.at[16]))
+    outs[3].start()
+    for cp in outs:
+        cp.wait()
+
+
+def cast_kernel(agg_h, eg_h, kg_h, vg_h, agg_o, emb_o, var_o, kg_o, vg_o, agg, eg, kg, vg, emb, var, kgf, vgf, sem):
+    def copy(n, src, dst):
+        cp = pltpu.make_async_copy(src, dst, sem.at[n])
+        cp.start()
+        return cp
+
+    first = [copy(0, vg_h, vg), copy(1, kg_h, kg), copy(2, eg_h, eg), copy(3, agg_h, agg)]
+    outs = []
+    for n, (src, full, dst) in enumerate(((vg, vgf, vg_o), (kg, kgf, kg_o))):
+        first[n].wait()
+        full[:, : D // 2] = src[:D].astype(f32)
+        full[:, D // 2 :] = src[D:].astype(f32)
+        outs.append(copy(4 + n, full, dst))
+    first[2].wait()
+    for g in range(2):
+        emb[g * VL : (g + 1) * VL] = eg[g * GR : g * GR + VL * PIX].astype(f32).reshape(VL, PIX, D)
+        var[g * VL : (g + 1) * VL] = eg[g * GR + VL * PIX : (g + 1) * GR].astype(f32)[:VL]
+    outs += [copy(6, emb, emb_o), copy(7, var, var_o)]
+    first[3].wait()
+    outs.append(copy(8, agg, agg_o))
     for cp in outs:
         cp.wait()
 
 
 def local(fields, var_ids, level_of, window_offset, w_embed, var_emb, w_key, w_value, w_out,
           latent_query, bias_table, lat_emb, d_aggregated):
-    smem = pl.BlockSpec(memory_space=pltpu.SMEM)
-    vmem = pl.BlockSpec(memory_space=pltpu.VMEM)
-    hbm = pl.BlockSpec(memory_space=pl.ANY)
+    hbm = pl.BlockSpec(memory_space=pltpu.HBM)
     dma = pltpu.SemaphoreType.DMA
 
     def v(*shape, dtype=bf16):
         return pltpu.VMEM(shape, dtype)
 
     scratch = [
-        v(NV, 2, 1024), v(240, PIX, D), v(256, D), v(D, D), v(D, D), v(D, D), dma((10,)),
+        pltpu.SMEM((240,), i32), pltpu.SMEM((240,), i32), pltpu.SMEM((1,), i32), pltpu.SMEM((H, 38), f32),
+        v(H, DH, dtype=f32), v(180, D), v(NV, 2, 1024), v(240, PIX, D), v(256, D), v(D, D), v(D, D), v(D, D), dma((17,)),
         v(8, 16, D), dma((7,)), dma((7,)),
         v(8, 16, D), v(8, 16, D), dma((7,)), dma((7,)),
-        v(8, 3, H, NP, dtype=f32), dma((7,)), dma((7,)),
+        v(8, 2, H, NP, dtype=f32), dma((7,)), dma((7,)),
+        v(8, H, NP, dtype=f32), dma((7,)), dma((7,)),
         v(8, 16, D), v(8, 16, D), dma((7,)), dma((7,)),
         v(8, 16, D), v(8, 16, D), dma((7,)), dma((7,)),
-        v(2 * D, D), v(D, D), v(3, 128, D), v(7, 16, D), v(D, D), v(128, D), v(2 * D, D),
+        v(2 * D, D // 2), v(D, D // 2), v(15, 32, D // 2), v(32, D // 2), v(D, D // 2), v(32, D // 2), v(2 * D, D // 2),
+        v(2 * D, D // 2), v(D, D // 2), v(15, 32, D // 2), v(32, D // 2), v(D, D // 2), v(32, D // 2), v(2 * D, D // 2),
         v(D, D), v(GR, D), v(3, 64, D), v(GR, D), v(D, D),
-        dma((22,)), dma((22,)), dma((8,)), dma((8,)),
+        dma((33,)), dma((33,)), dma((33,)), dma((33,)), dma((8,)), dma((8,)),
         v(D, D), v(D, D), v(D, D), v(D, D), v(2, D, GR), v(2, D, GR),
         v(2, GR, NP, dtype=f32), v(2, GR, NP),
     ]
     scratch += [v(H, 32, NP, dtype=f32)] * 4 + [v(NP, D)] + [v(H, 32, NP, dtype=f32)] * 3
     scratch += [v(H, D, NP), v(D, 2 * D), v(D, NP, dtype=f32)]
-    agg, eg, kv = pl.pallas_call(
+    agg, eg, kg, vg = pl.pallas_call(
         kernel,
         out_shape=[
             jax.ShapeDtypeStruct((16, D), bf16),
             jax.ShapeDtypeStruct((D, D), bf16),
-            jax.ShapeDtypeStruct((2 * D, D), bf16),
+            jax.ShapeDtypeStruct((2 * D, D // 2), bf16),
+            jax.ShapeDtypeStruct((2 * D, D // 2), bf16),
         ],
-        in_specs=[smem] * 4 + [hbm] * 6 + [vmem] * 2 + [hbm],
-        out_specs=[hbm] * 3,
+        in_specs=[hbm] * 13,
+        out_specs=[hbm] * 4,
         scratch_shapes=scratch,
         compiler_params=pltpu.CompilerParams(
-            collective_id=0, has_side_effects=True, vmem_limit_bytes=48 * 1024 * 1024
+            collective_id=0, has_side_effects=True, vmem_limit_bytes=62 * 1024 * 1024
         ),
     )(
-        var_ids, level_of, window_offset, bias_table,
+        var_ids, level_of, window_offset, bias_table.T,
         fields, w_embed, var_emb, w_key, w_value, w_out, latent_query, lat_emb,
         d_aggregated.reshape(16, D),
     )
-    eg = eg.reshape(2, GR, D)
-    embed = eg[:, : VL * PIX].astype(f32).reshape(NV, PIX, D)
-    var = eg[:, VL * PIX : GR - 1].astype(f32).reshape(NV, D)
-    kv = kv.astype(f32)
-    return agg.reshape(16, 1, D), embed, var, kv[:D], kv[D:]
+    agg, embed, var, key_grad, value_grad = pl.pallas_call(
+        cast_kernel,
+        out_shape=[
+            jax.ShapeDtypeStruct((16, D), bf16),
+            jax.ShapeDtypeStruct((NV, PIX, D), f32),
+            jax.ShapeDtypeStruct((NV, D), f32),
+            jax.ShapeDtypeStruct((D, D), f32),
+            jax.ShapeDtypeStruct((D, D), f32),
+        ],
+        in_specs=[hbm] * 4,
+        out_specs=[hbm] * 5,
+        scratch_shapes=[
+            v(16, D), v(D, D), v(2 * D, D // 2), v(2 * D, D // 2),
+            v(NV, PIX, D, dtype=f32), v(NV, D, dtype=f32), v(D, D, dtype=f32), v(D, D, dtype=f32),
+            dma((9,)),
+        ],
+        compiler_params=pltpu.CompilerParams(vmem_limit_bytes=62 * 1024 * 1024),
+    )(agg, eg, kg, vg)
+    return agg.reshape(16, 1, D), embed, var, key_grad, value_grad
 
 
 def solution(mesh):

time: 76 us -> 60.1 us (0.79)
  local copies, waits for them, and re-layouts: 12.3 us -> 0 us
  Pallas kernels: 60.9 us -> 58.6 us
  other arithmetic: 1.07 us -> 0 us
    unnamed x22 -> x0, local copies, waits for them, and re-layouts: 10 us -> none
    pallas_call x1, Pallas kernels: 60.9 us -> 55.8 us  [local(): pl.pallas_call(kernel, out_shape=[jax.ShapeDtypeStruct((16, D), bf16), ja...]
    pallas_call x0 -> x1, Pallas kernels: none -> 2.84 us  [local(): pl.pallas_call(cast_kernel, out_shape=[jax.ShapeDtypeStruct((16, D), bf16...]
    slice x2 -> x0, local copies, waits for them, and re-layouts: 1.64 us -> none  [the longest x1 1.61 us: local(): return (agg.reshape(16, 1, D), embed, var, kv[:D], kv[D:])]
    reshape x2 -> x0, other arithmetic: 1.07 us -> none  [the longest x1 1.07 us: local(): embed = eg[:, :VL * PIX].astype(f32).reshape(NV, PIX, D)]
where the time goes in v3:
time: 60.1 us; the launch traced here: 59.9 us
  Pallas kernels  58.6 us (98%)
  between operations  1.29 us (2%)
    pallas_call x1, Pallas kernels, local(): pl.pallas_call(kernel, out_shape=[jax.ShapeDtypeStruct((16, D), bf16), ja...  55.8 us
    pallas_call x1, Pallas kernels, local(): pl.pallas_call(cast_kernel, out_shape=[jax.ShapeDtypeStruct((16, D), bf16...  2.84 us

profile of v3, /device:TPU:1, one launch (start us, length us, event | category | flops | bytes accessed | tf_op | source)
XLA Modules:
  0.0 59.9 jit_solution(5151543955982885038)
XLA Ops:
  1.3 55.8 %shard_map.164 = (bf16[16,512]{1,0:T(8,128)(2,1)}, bf16[512,512]{1,0:T(8,128)(2,1)}, bf16[1024,256]{1,0:T(8,128)(2,1)}, bf16[1024,256]{1,0:T(8,128)(2,1)}) custom-call(s32[240]{0:T(256)} %ids_h.1, s32[240]{0:T(256)} %lvl_h.1, s32[1]{0:T(128)S(6)} %copy.18.off_h, f32[8,38]{1,0:T(8,128)} %bitcast.4, bf16[30,2,1024]{2,1,0:T(2,128)(2,1)} %fields_h.1, ...), custom_call_target="tpu_custom_call" | custom-call | tf_op jit(solution)/shard_map/pallas_call | solution.py:553
  57.1 2.8 %shard_map.165 = (bf16[16,512]{1,0:T(8,128)(2,1)}, f32[30,16,512]{2,1,0:T(8,128)}, f32[30,512]{1,0:T(8,128)}, f32[512,512]{1,0:T(8,128)}, f32[512,512]{1,0:T(8,128)}) custom-call(bf16[16,512]{1,0:T(8,128)(2,1)} %get-tuple-element.14.agg_h, bf16[512,512]{1,0:T(8,128)(2,1)} %get-tuple-element.15.eg_h, bf16[1024,256]{1,0:T(8,128)(2,1)} %get-tuple-element.16.kg_h, ...), custom_call_target="tpu_custom_call" | custom-call | tf_op jit(solution)/shard_map/pallas_call | solution.py:572

commit v4 on v3

--- a/solution.py
+++ b/solution.py
@@ -23,6 +23,15 @@
 def split(x):
     hi = x.astype(bf16)
     return hi, (x - hi.astype(f32)).astype(bf16)
+
+
+def hops(d):
+    return min(d, 4 - d)
+
+
+VAR = sorted(((a, b) for a in range(4) for b in range(2)), key=lambda o: -hops(o[0]) - 2 * o[1])[:-1]
+PATCH = sorted(((a, b) for a in range(4) for b in range(2)), key=lambda o: -hops(o[0]) - o[1] / 4)[:-1]
+SQUARE = sorted(((a, b) for a in range(4) for b in range(4)), key=lambda o: -hops(o[0]) - hops(o[1]))[:-1]
 
 
 def var_of(row):
@@ -44,12 +53,15 @@
     vb, vr1, vr2, vr3, vs1, vs2, vfin,
     egb, re1, re2, e1, fine,
     k_ss, k_rs, v_ss, v_rs, e_ss, e_rs,
-    wa, wat, wek, wev, wekt, wevt, ff, fb, bi, ss, sn, ga, gc, at, ca, cb, eb, fg, ctxt,
+    wa, wat, wot, wek, wev, wekt, wevt, ff, fb, bi, ss, sn, ga, gc, at, ca, cb, eb, fg, ctxt,
 ):
     i, j = lax.axis_index("var"), lax.axis_index("patch")
     z, xh = i // 2, i % 2
     y, c = j // 2, j % 2
     w_me = z * 4 + y
+    var_peers = [((z + a) % 4) * 2 + (xh + b) % 2 for a, b in VAR]
+    patch_peers = [((y + a) % 4) * 2 + (c + b) % 2 for a, b in PATCH]
+    square_peers = [((z + a) % 4, (y + b) % 4) for a, b in SQUARE]
 
     pending = []
 
@@ -99,20 +111,10 @@
         cp.start()
 
     barrier = pltpu.get_barrier_semaphore()
-    peers = [dict(var=(i + t) % 8) for t in range(1, 8)]
-    peers += [dict(patch=(j + t) % 8) for t in range(1, 8)]
-    peers += [
-        dict(var=((z + t) % 4) * 2 + xh, patch=((y + n) % 4) * 2 + c)
-        for t in range(1, 4)
-        for n in range(1, 4)
-    ]
+    peers = [dict(var=a * 2 + xh, patch=b * 2 + c) for (a, b), (d, e) in zip(square_peers, SQUARE) if d and e]
+    peers += [dict(var=n) for n in var_peers] + [dict(patch=n) for n in patch_peers]
     for dev in peers:
         pl.semaphore_signal(barrier, inc=1, device_id=dev, device_id_type=pl.DeviceIdType.MESH)
-    pl.semaphore_wait(barrier, len(peers))
-
-    xs = [remote(d_h, x_buf.at[i], x_ss.at[t - 1], x_rs.at[t - 1], var=(i + t) % 8) for t in range(1, 8)]
-    for cp in xs:
-        cp.start()
 
     for n in range(7, 13):
         local[n].wait()
@@ -144,6 +146,11 @@
         ff[g, VL * PIX :, :] = jnp.where(iota((16, NP), 0) < VL, 1.0, 0.0)
         fb[g] = ff[g].astype(bf16)
 
+    pl.semaphore_wait(barrier, len(peers))
+    xs = [remote(d_h, x_buf.at[i], x_ss.at[n], x_rs.at[n], var=peer) for n, peer in enumerate(var_peers)]
+    for cp in xs:
+        cp.start()
+
     local[1].wait()
 
     def gather_step(v, _):
@@ -164,29 +171,13 @@
     local[3].wait()
     local[4].wait()
     wat[...] = wa[...].T
+    local[5].wait()
+    wot[...] = wo[...].T
     wek[...] = dot(wa[...], wk[...]).astype(bf16)
     wev[...] = dot(wa[...], wv[...]).astype(bf16)
     for g in range(2):
         wekt[g] = wek[g * GR : (g + 1) * GR, :].T
         wevt[g] = wev[g * GR : (g + 1) * GR, :].T
-
-    local[5].wait()
-    local[6].wait()
-    for cp in xs:
-        cp.wait()
-    gx = dot(x_buf[...].reshape(NP, D), wo[...], NT).astype(bf16)
-    o = iota((NP, NP), 0)
-    src = ((o >> 1) & 7) * 16 + (o >> 4) * 2 + (o & 1)
-    perm = jnp.where(src == iota((NP, NP), 1), 1.0, 0.0).astype(bf16)
-    gs_rows = dot(perm, gx).astype(bf16)
-    g_snd[...] = gs_rows.reshape(8, 16, D)
-    gsends = []
-    for t in range(1, 8):
-        peer = (j + t) % 8
-        gsends.append(remote(g_snd.at[peer], g_buf.at[j], g_ss.at[t - 1], g_rs.at[t - 1], patch=peer))
-    for cp in gsends:
-        cp.start()
-    g_buf[j] = g_snd[j]
 
     spread_q = jnp.where((iota((DH, D), 1) & 63) == iota((DH, D), 0), 1.0, 0.0)
     qall = jnp.dot(q_v[...], spread_q, precision=lax.Precision.HIGHEST, preferred_element_type=f32)
@@ -211,7 +202,7 @@
 
     heads = jnp.where((iota((16, D), 1) >> 6) == iota((16, D), 0), 1.0, 0.0).astype(bf16)
     tile_row = iota((16, NP), 0)
-    for g in range(2):
+    def square_sums(g):
         ones = ff[g, VL * PIX :, :]
         for t in range(8):
             cols = []
@@ -232,6 +223,26 @@
             ss[:, g * 16 + 2 * t, :] = sq[:H, :NP]
             ss[:, g * 16 + 2 * t + 1, :] = sq[:H, NP:]
 
+
+    square_sums(0)
+
+    local[6].wait()
+    for cp in xs:
+        cp.wait()
+    gx = dot(x_buf[...].reshape(NP, D), wot[...]).astype(bf16)
+    o = iota((NP, NP), 0)
+    src = ((o >> 1) & 7) * 16 + (o >> 4) * 2 + (o & 1)
+    perm = jnp.where(src == iota((NP, NP), 1), 1.0, 0.0).astype(bf16)
+    gs_rows = dot(perm, gx).astype(bf16)
+    g_snd[...] = gs_rows.reshape(8, 16, D)
+    gsends = []
+    for n, peer in enumerate(patch_peers):
+        gsends.append(remote(g_snd.at[peer], g_buf.at[j], g_ss.at[n], g_rs.at[n], patch=peer))
+    for cp in gsends:
+        cp.start()
+    g_buf[j] = g_snd[j]
+
+    square_sums(1)
     scale = DH**-0.5
     slot = iota((H, 32, NP), 1)
     real = (slot & 15) < VL
@@ -244,8 +255,8 @@
     ml_buf[i, 0] = m[:, 0, :]
     ml_buf[i, 1] = jnp.sum(e, axis=1)
     mls = [
-        remote(ml_buf.at[i], ml_buf.at[i], ml_ss.at[t - 1], ml_rs.at[t - 1], var=(i + t) % 8)
-        for t in range(1, 8)
+        remote(ml_buf.at[i], ml_buf.at[i], ml_ss.at[n], ml_rs.at[n], var=peer)
+        for n, peer in enumerate(var_peers)
     ]
     for cp in mls:
         cp.start()
@@ -275,8 +286,8 @@
             ga[2 * pair + 1, g * 16 : (g + 1) * 16, :] = got[:, NP:]
     r_buf[i] = jnp.sum(at[...] * ga[...], axis=1)
     rss = [
-        remote(r_buf.at[i], r_buf.at[i], r_ss.at[t - 1], r_rs.at[t - 1], var=(i + t) % 8)
-        for t in range(1, 8)
+        remote(r_buf.at[i], r_buf.at[i], r_ss.at[n], r_rs.at[n], var=peer)
+        for n, peer in enumerate(var_peers)
     ]
     for cp in rss:
         cp.start()
@@ -307,16 +318,15 @@
         cp.start()
         return cp
 
-    def at16(w):
-        return dict(var=(w // 4) * 2 + xh, patch=(w % 4) * 2 + c)
-
     def core_sum_end(cp, buf, r1, s1, r2, s_sem, r_sem):
         cp.wait()
         s1[...] = (buf[pl.ds(c * D, D), :].astype(f32) + r1[...].astype(f32)).astype(bf16)
         cps = []
-        for t in range(1, 16):
-            w = (w_me + t) % 16
-            cps.append(remote(s1.at[pl.ds(w * 32, 32)], r2.at[t - 1], s_sem.at[t], r_sem.at[t], **at16(w)))
+        for n, (a, b) in enumerate(square_peers):
+            part = s1.at[pl.ds((a * 4 + b) * 32, 32)]
+            cps.append(
+                remote(part, r2.at[n], s_sem.at[n + 1], r_sem.at[n + 1], var=a * 2 + xh, patch=b * 2 + c)
+            )
         for cp in cps:
             cp.start()
         return cps
@@ -338,8 +348,10 @@
         fin[pl.ds(row, 32), :] = (s2[...].astype(f32) + r3[...].astype(f32)).astype(bf16)
         rows = fin.at[pl.ds(row, 32)]
         cps = []
-        for t in range(1, 16):
-            cps.append(remote(rows, rows, s_sem.at[16 + t], r_sem.at[16 + t], **at16((w_me + t) % 16)))
+        for n, (a, b) in enumerate(square_peers):
+            cps.append(
+                remote(rows, rows, s_sem.at[17 + n], r_sem.at[17 + n], var=a * 2 + xh, patch=b * 2 + c)
+            )
         for cp in cps:
             cp.start()
         return cps
@@ -372,19 +384,6 @@
     put(vb, dot(wat[...], fg[:, D:]).astype(bf16))
     v1 = core_sum_start(vb, vr1, v_ss, v_rs)
 
-    for h in range(H):
-        acc = dot(wevt[0, h * DH : (h + 1) * DH, :], eb[h, :GR, :])
-        acc = acc + dot(wevt[1, h * DH : (h + 1) * DH, :], eb[h, GR:, :])
-        ctxt[h * DH : (h + 1) * DH, :] = acc
-    c_snd[...] = ctxt[...].T.astype(bf16).reshape(8, 16, D)
-    cs = []
-    for t in range(1, 8):
-        peer = (i + t) % 8
-        cs.append(remote(c_snd.at[peer], c_buf.at[i], c_ss.at[t - 1], c_rs.at[t - 1], var=peer))
-    v2 = core_sum_end(v1, vb, vr1, vs1, vr2, v_ss, v_rs)
-    for cp in cs:
-        cp.start()
-    c_buf[i] = c_snd[i]
 
     for cp in rss:
         cp.wait()
@@ -415,13 +414,26 @@
             fg[g * GR : (g + 1) * GR, lanes] = total.astype(bf16)
     put(kb, dot(wat[...], fg[:, :D]).astype(bf16))
     k1 = core_sum_start(kb, kr1, k_ss, k_rs)
+    v2 = core_sum_end(v1, vb, vr1, vs1, vr2, v_ss, v_rs)
+    k2 = core_sum_end(k1, kb, kr1, ks1, kr2, k_ss, k_rs)
     for g in range(2):
         rows = slice(g * GR, (g + 1) * GR)
         egb[rows, :] = (dot(fg[rows, :D], wk[...], NT) + dot(fg[rows, D:], wv[...], NT)).astype(bf16)
     ex1 = remote(egb.at[pl.ds((1 - c) * GR, GR)], re1, e_ss.at[0], e_rs.at[0], patch=sib)
     ex1.start()
 
-    k2 = core_sum_end(k1, kb, kr1, ks1, kr2, k_ss, k_rs)
+    for h in range(H):
+        acc = dot(wevt[0, h * DH : (h + 1) * DH, :], eb[h, :GR, :])
+        acc = acc + dot(wevt[1, h * DH : (h + 1) * DH, :], eb[h, GR:, :])
+        ctxt[h * DH : (h + 1) * DH, :] = acc
+    c_snd[...] = ctxt[...].T.astype(bf16).reshape(8, 16, D)
+    cs = []
+    for n, peer in enumerate(var_peers):
+        cs.append(remote(c_snd.at[peer], c_buf.at[i], c_ss.at[n], c_rs.at[n], var=peer))
+    for cp in cs:
+        cp.start()
+    c_buf[i] = c_snd[i]
+
     ex1.wait()
     e1[...] = (egb[pl.ds(c * GR, GR), :].astype(f32) + re1[...].astype(f32)).astype(bf16)
     ex2 = []
@@ -433,6 +445,24 @@
     for cp in ex2:
         cp.start()
 
+    v3 = zy_sum_end(v2, vs1, vr2, vs2, vr3, v_ss, v_rs)
+    k3 = zy_sum_end(k2, ks1, kr2, ks2, kr3, k_ss, k_rs)
+    v4 = x_sum_end(v3, vs2, vr3, vfin, v_ss, v_rs)
+    for cp in ex2:
+        cp.wait()
+    tot = e1[pl.ds(y * 64, 64), :].astype(f32)
+    for n in range(3):
+        tot = tot + re2[n].astype(f32)
+    erow = c * GR + y * 64
+    fine[pl.ds(erow, 64), :] = tot.astype(bf16)
+    ex3 = []
+    for t in range(1, 4):
+        peer = (y + t) % 4
+        own_rows = fine.at[pl.ds(erow, 64)]
+        ex3.append(remote(own_rows, own_rows, e_ss.at[3 + t], e_rs.at[3 + t], patch=peer * 2 + c))
+    for cp in ex3:
+        cp.start()
+    k4 = x_sum_end(k3, ks2, kr3, kfin, k_ss, k_rs)
     for cp in cs:
         cp.wait()
     cx = c_buf[0].astype(f32)
@@ -446,36 +476,17 @@
     take = ((r >= 0) & (r < 2)) & (iota((NP, 16), 1) == r * 8 + (dst >> 4))
     a_snd[...] = dot(jnp.where(take, 1.0, 0.0).astype(bf16), agg).astype(bf16).reshape(8, 16, D)
     sends = []
-    for t in range(1, 8):
-        peer = (j + t) % 8
-        sends.append(remote(a_snd.at[peer], a_buf.at[j], a_ss.at[t - 1], a_rs.at[t - 1], patch=peer))
+    for n, peer in enumerate(patch_peers):
+        sends.append(remote(a_snd.at[peer], a_buf.at[j], a_ss.at[n], a_rs.at[n], patch=peer))
     for cp in sends:
         cp.start()
     a_buf[j] = a_snd[j]
 
-    v3 = zy_sum_end(v2, vs1, vr2, vs2, vr3, v_ss, v_rs)
-    for cp in ex2:
-        cp.wait()
-    tot = e1[pl.ds(y * 64, 64), :].astype(f32)
-    for n in range(3):
-        tot = tot + re2[n].astype(f32)
-    erow = c * GR + y * 64
-    fine[pl.ds(erow, 64), :] = tot.astype(bf16)
-    ex3 = []
-    for t in range(1, 4):
-        peer = (y + t) % 4
-        own_rows = fine.at[pl.ds(erow, 64)]
-        ex3.append(remote(own_rows, own_rows, e_ss.at[3 + t], e_rs.at[3 + t], patch=peer * 2 + c))
-    for cp in ex3:
-        cp.start()
-    v4 = x_sum_end(v3, vs2, vr3, vfin, v_ss, v_rs)
-    k3 = zy_sum_end(k2, ks1, kr2, ks2, kr3, k_ss, k_rs)
     for cp in ex3:
         cp.wait()
     half = fine.at[pl.ds(c * GR, GR)]
     ex4 = remote(half, half, e_ss.at[7], e_rs.at[7], patch=sib)
     ex4.start()
-    k4 = x_sum_end(k3, ks2, kr3, kfin, k_ss, k_rs)
 
     for cp in sends:
         cp.wait()
@@ -545,7 +556,7 @@
         v(2 * D, D // 2), v(D, D // 2), v(15, 32, D // 2), v(32, D // 2), v(D, D // 2), v(32, D // 2), v(2 * D, D // 2),
         v(D, D), v(GR, D), v(3, 64, D), v(GR, D), v(D, D),
         dma((33,)), dma((33,)), dma((33,)), dma((33,)), dma((8,)), dma((8,)),
-        v(D, D), v(D, D), v(D, D), v(D, D), v(2, D, GR), v(2, D, GR),
+        v(D, D), v(D, D), v(D, D), v(D, D), v(D, D), v(2, D, GR), v(2, D, GR),
         v(2, GR, NP, dtype=f32), v(2, GR, NP),
     ]
     scratch += [v(H, 32, NP, dtype=f32)] * 4 + [v(NP, D)] + [v(H, 32, NP, dtype=f32)] * 3

time: 60.1 us -> 57.4 us (0.955)
  Pallas kernels: 58.6 us -> 55.9 us
    pallas_call x1, Pallas kernels: 55.8 us -> 53.1 us  [local(): pl.pallas_call(kernel, out_shape=[jax.ShapeDtypeStruct((16, D), bf16), ja...]
where the time goes in v4:
time: 57.4 us; the launch traced here: 57.2 us
  Pallas kernels  55.9 us (97%)
  between operations  1.29 us (2%)
    pallas_call x1, Pallas kernels, local(): pl.pallas_call(kernel, out_shape=[jax.ShapeDtypeStruct((16, D), bf16), ja...  53.1 us
    pallas_call x1, Pallas kernels, local(): pl.pallas_call(cast_kernel, out_shape=[jax.ShapeDtypeStruct((16, D), bf16...  2.84 us

profile of v4, /device:TPU:1, one launch (start us, length us, event | category | flops | bytes accessed | tf_op | source)
XLA Modules:
  0.0 57.2 jit_solution(13299403853967535902)
XLA Ops:
  1.3 53.1 %shard_map.164 = (bf16[16,512]{1,0:T(8,128)(2,1)}, bf16[512,512]{1,0:T(8,128)(2,1)}, bf16[1024,256]{1,0:T(8,128)(2,1)}, bf16[1024,256]{1,0:T(8,128)(2,1)}) custom-call(s32[240]{0:T(256)} %ids_h.1, s32[240]{0:T(256)} %lvl_h.1, s32[1]{0:T(128)S(6)} %copy.18.off_h, f32[8,38]{1,0:T(8,128)} %bitcast.4, bf16[30,2,1024]{2,1,0:T(2,128)(2,1)} %fields_h.1, ...), custom_call_target="tpu_custom_call" | custom-call | tf_op jit(solution)/shard_map/pallas_call | solution.py:564
  54.4 2.8 %shard_map.165 = (bf16[16,512]{1,0:T(8,128)(2,1)}, f32[30,16,512]{2,1,0:T(8,128)}, f32[30,512]{1,0:T(8,128)}, f32[512,512]{1,0:T(8,128)}, f32[512,512]{1,0:T(8,128)}) custom-call(bf16[16,512]{1,0:T(8,128)(2,1)} %get-tuple-element.14.agg_h, bf16[512,512]{1,0:T(8,128)(2,1)} %get-tuple-element.15.eg_h, bf16[1024,256]{1,0:T(8,128)(2,1)} %get-tuple-element.16.kg_h, ...), custom_call_target="tpu_custom_call" | custom-call | tf_op jit(solution)/shard_map/pallas_call | solution.py:583

commit v5 on v4

--- a/solution.py
+++ b/solution.py
@@ -170,14 +170,12 @@
         wa[g * GR + VL * PIX : (g + 1) * GR, :] = dot(hot, vem[...]).astype(bf16)
     local[3].wait()
     local[4].wait()
-    wat[...] = wa[...].T
     local[5].wait()
     wot[...] = wo[...].T
     wek[...] = dot(wa[...], wk[...]).astype(bf16)
     wev[...] = dot(wa[...], wv[...]).astype(bf16)
     for g in range(2):
         wekt[g] = wek[g * GR : (g + 1) * GR, :].T
-        wevt[g] = wev[g * GR : (g + 1) * GR, :].T
 
     spread_q = jnp.where((iota((DH, D), 1) & 63) == iota((DH, D), 0), 1.0, 0.0)
     qall = jnp.dot(q_v[...], spread_q, precision=lax.Precision.HIGHEST, preferred_element_type=f32)
@@ -291,6 +289,9 @@
     ]
     for cp in rss:
         cp.start()
+    wat[...] = wa[...].T
+    for g in range(2):
+        wevt[g] = wev[g * GR : (g + 1) * GR, :].T
     for cp in mls:
         cp.wait()
     mall = ml_buf[0, 0]
@@ -416,11 +417,24 @@
     k1 = core_sum_start(kb, kr1, k_ss, k_rs)
     v2 = core_sum_end(v1, vb, vr1, vs1, vr2, v_ss, v_rs)
     k2 = core_sum_end(k1, kb, kr1, ks1, kr2, k_ss, k_rs)
-    for g in range(2):
-        rows = slice(g * GR, (g + 1) * GR)
+    def embed_grad(g):
+        rows = pl.ds(pl.multiple_of(g * GR, GR), GR)
         egb[rows, :] = (dot(fg[rows, :D], wk[...], NT) + dot(fg[rows, D:], wv[...], NT)).astype(bf16)
+
+    embed_grad(1 - c)
     ex1 = remote(egb.at[pl.ds((1 - c) * GR, GR)], re1, e_ss.at[0], e_rs.at[0], patch=sib)
     ex1.start()
+    embed_grad(c)
+    ex1.wait()
+    e1[...] = (egb[pl.ds(c * GR, GR), :].astype(f32) + re1[...].astype(f32)).astype(bf16)
+    ex2 = []
+    for t in range(1, 4):
+        peer = (y + t) % 4
+        ex2.append(
+            remote(e1.at[pl.ds(peer * 64, 64)], re2.at[t - 1], e_ss.at[t], e_rs.at[t], patch=peer * 2 + c)
+        )
+    for cp in ex2:
+        cp.start()
 
     for h in range(H):
         acc = dot(wevt[0, h * DH : (h + 1) * DH, :], eb[h, :GR, :])
@@ -433,17 +447,6 @@
     for cp in cs:
         cp.start()
     c_buf[i] = c_snd[i]
-
-    ex1.wait()
-    e1[...] = (egb[pl.ds(c * GR, GR), :].astype(f32) + re1[...].astype(f32)).astype(bf16)
-    ex2 = []
-    for t in range(1, 4):
-        peer = (y + t) % 4
-        ex2.append(
-            remote(e1.at[pl.ds(peer * 64, 64)], re2.at[t - 1], e_ss.at[t], e_rs.at[t], patch=peer * 2 + c)
-        )
-    for cp in ex2:
-        cp.start()
 
     v3 = zy_sum_end(v2, vs1, vr2, vs2, vr3, v_ss, v_rs)
     k3 = zy_sum_end(k2, ks1, kr2, ks2, kr3, k_ss, k_rs)
@@ -496,17 +499,22 @@
     a_snd[0] = acc.astype(bf16)
     outs = [pltpu.make_async_copy(a_snd.at[0], agg_o, lsem.at[13])]
     outs[0].start()
+    def store(ref, out, side, rows, n):
+        part = pl.ds(side * rows, rows)
+        outs.append(pltpu.make_async_copy(ref.at[part], out.at[part], lsem.at[n]))
+        outs[-1].start()
+
+    store(fine, eg_o, c, GR, 14)
     ex4.wait()
-    outs.append(pltpu.make_async_copy(fine, eg_o, lsem.at[14]))
-    outs[1].start()
+    store(fine, eg_o, 1 - c, GR, 15)
     v5 = gather_end(v4, vfin, v_ss, v_rs)
+    store(vfin, vg_o, c, D, 16)
+    k5 = gather_end(k4, kfin, k_ss, k_rs)
+    store(kfin, kg_o, c, D, 17)
     v5.wait()
-    outs.append(pltpu.make_async_copy(vfin, vg_o, lsem.at[15]))
-    outs[2].start()
-    k5 = gather_end(k4, kfin, k_ss, k_rs)
+    store(vfin, vg_o, 1 - c, D, 18)
     k5.wait()
-    outs.append(pltpu.make_async_copy(kfin, kg_o, lsem.at[16]))
-    outs[3].start()
+    store(kfin, kg_o, 1 - c, D, 19)
     for cp in outs:
         cp.wait()
 
@@ -545,7 +553,7 @@
 
     scratch = [
         pltpu.SMEM((240,), i32), pltpu.SMEM((240,), i32), pltpu.SMEM((1,), i32), pltpu.SMEM((H, 38), f32),
-        v(H, DH, dtype=f32), v(180, D), v(NV, 2, 1024), v(240, PIX, D), v(256, D), v(D, D), v(D, D), v(D, D), dma((17,)),
+        v(H, DH, dtype=f32), v(180, D), v(NV, 2, 1024), v(240, PIX, D), v(256, D), v(D, D), v(D, D), v(D, D), dma((20,)),
         v(8, 16, D), dma((7,)), dma((7,)),
         v(8, 16, D), v(8, 16, D), dma((7,)), dma((7,)),
         v(8, 2, H, NP, dtype=f32), dma((7,)), dma((7,)),

time: 57.4 us -> 56.4 us (0.983)
  Pallas kernels: 55.9 us -> 55 us
    pallas_call x1, Pallas kernels: 53.1 us -> 52.2 us  [local(): pl.pallas_call(kernel, out_shape=[jax.ShapeDtypeStruct((16, D), bf16), ja...]
where the time goes in v5:
time: 56.4 us; the launch traced here: 56.3 us
  Pallas kernels  55 us (98%)
  between operations  1.29 us (2%)
    pallas_call x1, Pallas kernels, local(): pl.pallas_call(kernel, out_shape=[jax.ShapeDtypeStruct((16, D), bf16), ja...  52.2 us
    pallas_call x1, Pallas kernels, local(): pl.pallas_call(cast_kernel, out_shape=[jax.ShapeDtypeStruct((16, D), bf16...  2.84 us

profile of v5, /device:TPU:1, one launch (start us, length us, event | category | flops | bytes accessed | tf_op | source)
XLA Modules:
  0.0 56.3 jit_solution(14838015382859067854)
XLA Ops:
  1.3 52.2 %shard_map.164 = (bf16[16,512]{1,0:T(8,128)(2,1)}, bf16[512,512]{1,0:T(8,128)(2,1)}, bf16[1024,256]{1,0:T(8,128)(2,1)}, bf16[1024,256]{1,0:T(8,128)(2,1)}) custom-call(s32[240]{0:T(256)} %ids_h.1, s32[240]{0:T(256)} %lvl_h.1, s32[1]{0:T(128)S(6)} %copy.18.off_h, f32[8,38]{1,0:T(8,128)} %bitcast.4, bf16[30,2,1024]{2,1,0:T(2,128)(2,1)} %fields_h.1, ...), custom_call_target="tpu_custom_call" | custom-call | tf_op jit(solution)/shard_map/pallas_call | solution.py:572
  53.4 2.8 %shard_map.165 = (bf16[16,512]{1,0:T(8,128)(2,1)}, f32[30,16,512]{2,1,0:T(8,128)}, f32[30,512]{1,0:T(8,128)}, f32[512,512]{1,0:T(8,128)}, f32[512,512]{1,0:T(8,128)}) custom-call(bf16[16,512]{1,0:T(8,128)(2,1)} %get-tuple-element.14.agg_h, bf16[512,512]{1,0:T(8,128)(2,1)} %get-tuple-element.15.eg_h, bf16[1024,256]{1,0:T(8,128)(2,1)} %get-tuple-element.16.kg_h, ...), custom_call_target="tpu_custom_call" | custom-call | tf_op jit(solution)/shard_map/pallas_call | solution.py:591
